TPU v7x, 32 devices: a whole 2x2x4 slice. The times are simulated.
32 devices in a mesh: req: 8 (over z, x), tp: 4 (over y, core).
Axes of the slice: x: 2, y: 2, z: 4, core: 2. Of those that a mesh axis runs over, the one named last changes fastest.
Arguments:
- patches: bfloat16 [8192, 1408], P('req')
- segment_ids: int32 [8192], P('req'), may hold values from 0 to 15, as said below
- grid_sides: int32 [8192], P('req'), may hold values from 8 to 32, as said below
- split_plan: int32 [8, 2], P('req'), may hold values from 0 to 960, as said below
- owner_dev: int32 [2048], P('req'), may hold values from 0 to 7, as said below
- dest_row: int32 [2048], P('req'), may hold values from 0 to 255, as said below
- ln_gain: float32 [1408], replicated, may hold values from 0.25 to 1.75
- ln_bias: float32 [1408], replicated, may hold values from -3 to 3
- w_qkv: bfloat16 [3, 1408, 1408], P(None, 'tp')
- w_out: bfloat16 [1408, 1408], P('tp'), may hold values from -0.625 to 0.625
- w_proj: bfloat16 [5632, 2048], P(None, 'tp'), may hold values from -0.078125 to 0.078125
Outputs:
- vision_tokens: bfloat16 [2048, 2048], P('req', 'tp')
Inputs may be any that keep to these rules, and one draw needn't show every extreme that they name: `segment_ids`: within each packed row the ids start at 0, never fall, and one id's patches are contiguous; an image with grid side s has s * s patches (the last image of the whole packing may be cut short) and lies in at most two neighbouring rows. `grid_sides`: all patches of one image share its grid side, a multiple of 8. split_plan[r, 0] is the number of patches of row r's first image that lie in row r - 1, split_plan[r, 1] the number of patches of row r's last image that lie in row r + 1; both are 0 where no image crosses. `owner_dev`: the merged tokens of one row form blocks of 64 consecutive merged tokens; each block goes whole to one owner, a row's blocks go to different owners, and every owner receives 1024 // 4 merged tokens. `dest_row`: every row of every owner's output receives exactly one merged token.
All inputs are finite; a program needn't handle non-finite values.
Results may differ from a plain program's by a relative error of at most 0.019.
Values may be sent and summed in bfloat16 or wider, within the bound.
A program may use at most 128 MiB of HBM per device.

v0:
```python
import jax
import jax.numpy as jnp
from jax import lax
from jax.sharding import PartitionSpec as P

HD = 88


def extended(value, sides, width):
    for axis, dim in sides:
        count, length = (lax.axis_size(axis), value.shape[dim])
        up = [(i, (i + 1) % count) for i in range(count - 1)]
        down = [(j, i) for i, j in up]
        last = lax.slice_in_dim(value, length - width, length, axis=dim)
        leading = lax.slice_in_dim(value, 0, width, axis=dim)
        before = lax.ppermute(last, axis, up)
        after = lax.ppermute(leading, axis, down)
        value = jnp.concatenate([before, value, after], axis=dim)
    return value


def layer_norm(inputs, scale_vec, shift_vec):
    widened = inputs.astype(jnp.float32)
    centred = widened - jnp.mean(widened, axis=-1, keepdims=True)
    variance = jnp.mean(centred * centred, axis=-1, keepdims=True)
    return (centred * lax.rsqrt(variance + 1e-06) * scale_vec + shift_vec).astype(jnp.bfloat16)


def grid_positions(seg_row, side_row, first_offset):
    row_len = seg_row.shape[0]
    tok_index = jnp.arange(row_len, dtype=jnp.int32)
    boundary = jnp.concatenate([jnp.ones((1,), dtype=bool), seg_row[1:] != seg_row[:-1]])
    seg_start = lax.cummax(jnp.where(boundary, tok_index, 0), axis=0)
    offset = tok_index - seg_start + jnp.where(seg_row == 0, first_offset, 0)
    half_side = side_row // 2
    window = offset // 4
    corner = offset % 4
    return (2 * (window // half_side) + corner // 2, 2 * (window % half_side) + corner % 2)


def key_labels(seg_row, plan_row):
    row_len = seg_row.shape[0]
    tok_index = jnp.arange(row_len, dtype=jnp.int32)
    before = jnp.where(tok_index >= row_len - plan_row[0], 0, -1).astype(jnp.int32)
    after_keys = jnp.where(tok_index < plan_row[1], seg_row[row_len - 1], -1)
    return jnp.concatenate([before, seg_row, after_keys])


def rotate_pairs(channels, angles, axis_pos):
    quarter = channels.shape[axis_pos] // 2
    first_half = lax.slice_in_dim(channels, 0, quarter, axis=axis_pos)
    second_half = lax.slice_in_dim(channels, quarter, 2 * quarter, axis=axis_pos)
    cosine = jnp.cos(angles)
    sine_tab = jnp.sin(angles)
    return jnp.concatenate(
        [
            first_half * cosine - second_half * sine_tab,
            second_half * cosine + first_half * sine_tab,
        ],
        axis=axis_pos,
    )


def apply_rope(channels, row_angles, col_angles, axis_pos):
    half_width = channels.shape[axis_pos] // 2
    row_part = rotate_pairs(
        lax.slice_in_dim(channels, 0, half_width, axis=axis_pos), row_angles, axis_pos
    )
    col_part = rotate_pairs(
        lax.slice_in_dim(channels, half_width, 2 * half_width, axis=axis_pos), col_angles, axis_pos
    )
    return jnp.concatenate([row_part, col_part], axis=axis_pos)


def on_device(
    patches,
    segment_ids,
    grid_sides,
    split_plan,
    owner_dev,
    dest_row,
    ln_gain,
    ln_bias,
    w_qkv,
    w_out,
    w_proj,
):
    tok_count = patches.shape[0]
    feat_width = patches.shape[1]
    local_width = w_qkv.shape[1]
    local_heads = local_width // HD
    normed = layer_norm(patches, ln_gain, ln_bias)
    mixed_qkv = jnp.einsum("td,kcd->kct", normed, w_qkv, preferred_element_type=jnp.float32)
    grid_row, grid_col = grid_positions(segment_ids, grid_sides, split_plan[0, 0])
    quarter = HD // 4
    frequency = 10000.0 ** (-jnp.arange(quarter, dtype=jnp.float32) / quarter)
    row_angles = frequency[:, None] * grid_row.astype(jnp.float32)[None, :]
    col_angles = frequency[:, None] * grid_col.astype(jnp.float32)[None, :]
    shaped = mixed_qkv.reshape(3, local_heads, HD, tok_count)
    queries = apply_rope(shaped[0], row_angles, col_angles, 1).astype(jnp.bfloat16)
    key_rot = apply_rope(shaped[1], row_angles, col_angles, 1)
    key_value = jnp.stack([key_rot, shaped[2]]).astype(jnp.bfloat16)
    near_kv = extended(key_value, (("req", 3),), tok_count)
    near_keys = near_kv[0]
    near_values = near_kv[1]
    labels = key_labels(segment_ids, split_plan[0])
    block_rows = min(512, tok_count)
    w_heads = w_out.reshape(local_heads, HD, feat_width)

    def attend_block(first_row):
        q_block = lax.dynamic_slice_in_dim(queries, first_row, block_rows, 2)
        seg_block = lax.dynamic_slice_in_dim(segment_ids, first_row, block_rows, 0)
        allowed = seg_block[:, None] == labels[None, :]
        scores = jnp.einsum(
            "hcq,hck->hqk", q_block, near_keys, preferred_element_type=jnp.float32
        ) * HD ** (-0.5)
        scores = jnp.where(allowed[None], scores, -1e30)
        largest = jnp.max(scores, axis=-1, keepdims=True)
        weights = jnp.exp(scores - largest)
        attn_probs = (weights / jnp.sum(weights, axis=-1, keepdims=True)).astype(jnp.bfloat16)
        heads_out = jnp.einsum(
            "hqk,hck->hcq", attn_probs, near_values, preferred_element_type=jnp.float32
        ).astype(jnp.bfloat16)
        return jnp.einsum("hcq,hcd->qd", heads_out, w_heads, preferred_element_type=jnp.float32)

    block_starts = jnp.arange(tok_count // block_rows, dtype=jnp.int32) * block_rows
    partial_value = lax.map(attend_block, block_starts).reshape(tok_count, feat_width)
    attn_sum = lax.psum(partial_value.astype(jnp.bfloat16), "tp").astype(jnp.float32)
    mixed_rows = (patches.astype(jnp.float32) + attn_sum).astype(jnp.bfloat16)
    merged = mixed_rows.reshape(tok_count // 4, 4 * feat_width)
    projected = jnp.dot(merged, w_proj, preferred_element_type=jnp.float32).astype(jnp.bfloat16)
    per_owner = owner_dev.shape[0]
    peer_count = lax.axis_size("req")
    owner_slots = 2 * per_owner // peer_count
    matches = (owner_dev[:, None] == jnp.arange(peer_count, dtype=jnp.int32)[None, :]).astype(
        jnp.int32
    )
    arrival = jnp.sum(jnp.cumsum(matches, axis=0) * matches, axis=1) - 1
    send_slot = owner_dev * owner_slots + arrival
    out_cols = projected.shape[1]
    send_rows = (
        jnp.zeros((peer_count * owner_slots, out_cols), jnp.bfloat16).at[send_slot].set(projected)
    )
    send_dest = (
        jnp.full((peer_count * owner_slots,), per_owner, jnp.int32).at[send_slot].set(dest_row)
    )
    got_rows, got_dest = (
        lax.all_to_all(send_rows, "req", split_axis=0, concat_axis=0, tiled=True),
        lax.all_to_all(send_dest, "req", split_axis=0, concat_axis=0, tiled=True),
    )
    return jnp.zeros((per_owner, out_cols), jnp.bfloat16).at[got_dest].set(got_rows, mode="drop")


def solution(mesh):
    placed = (
        P("req", None),
        P("req"),
        P("req"),
        P("req", None),
        P("req"),
        P("req"),
        P(),
        P(),
        P(None, "tp", None),
        P("tp", None),
        P(None, "tp"),
    )
    return jax.shard_map(
        on_device, mesh=mesh, in_specs=placed, out_specs=P("req", "tp"), check_vma=False
    )
```

profile of v0, /device:TPU:0, one launch (start us, length us, event | category | flops | bytes accessed | tf_op | source)
XLA Modules:
  0.0 276.0 jit_solution(14019508457941081962)
XLA Ops:
  6.6 2.4 convert_reduce_fusion
  10.3 3.8 %fusion.38 = f32[3,352,1024]{2,1,0:T(8,128)S(1)} fusion(bf16[3,352,1408]{2,1,0:T(8,128)(2,1)S(1)} %copy-done, bf16[1024,1408]{1,0:T(8,128)(2,1)S(1)} %copy-done.2, f32[1408]{0:T(1024)S(1)} %copy-done.9, f32[1408]{0:T(1024)S(1)} %copy-done.10, f32[1024]{0:T(1024)S(1)} %add_rsqrt_fusion, f32[1024]{0:T(1024)S(1)} %broadcast_multiply_fusion), kind=kOutput, calls=%fused_computation.42 | convolution fusion | flops 3053715456 | bytes 10202112 | tf_op jit(solution)/shard_map/td,kcd->kct/dot_general | solution.py:93
  14.1 1.4 fusion.70
  18.6 1.8 subtract_convert_fusion.1
  21.8 5.9 %collective-permute-start = (bf16[2,4,88,1024]{3,2,1,0:T(8,128)(2,1)}, bf16[2,4,88,1024]{3,2,1,0:T(8,128)(2,1)}, u32[]{:S(2)}, u32[]{:S(2)}) collective-permute-start(bf16[2,4,88,1024]{3,2,1,0:T(8,128)(2,1)} %pad_maximum_fusion.1), channel_id=1, source_target_pairs={{0,4},{4,8},{8,12},{12,16},{16,20},{20,24},{24,28},{1,5},{5,9},{9,... | collective-permute-start | bytes 4325384 | tf_op jit(solution)/shard_map/ppermute | solution.py:16
  27.7 1.3 collective-permute-start.1
  32.9 55.8 %collective-permute-done = bf16[2,4,88,1024]{3,2,1,0:T(8,128)(2,1)} collective-permute-done((bf16[2,4,88,1024]{3,2,1,0:T(8,128)(2,1)}, bf16[2,4,88,1024]{3,2,1,0:T(8,128)(2,1)}, u32[]{:S(2)}, u32[]{:S(2)}) %collective-permute-start) | collective-permute-done | bytes 1441824 | tf_op jit(solution)/shard_map/ppermute | solution.py:16
  88.7 2.0 pad_maximum_fusion
  90.6 2.5 slice_bitcast_fusion
  93.1 69.2 %while.10 = (s32[]{:T(128)}, bf16[2,512,1408]{2,1,0:T(8,128)(2,1)}, s32[2]{0:T(128)S(1)}, s32[1024]{0:T(1024)S(1)}, s32[3072]{0:T(1024)S(1)}, /*index=5*/bf16[4,...) while((s32[]{:T(128)}, bf16[2,512,1408]{2,1,0:T(8,128)(2,1)}, ...), condition=%wide.region_11.12_spmd, body=%wide.region_8.11_spmd.sunk | while | flops 2761608192 | bytes 62073512 | solution.py:127
  96.8 15.8 %fusion.89 = (f32[4,512]{1,0:T(4,128)S(1)}, f32[4,512,3072]{2,1,0:T(8,128)}) fusion(pred[512,3072]{1,0:T(8,128)(4,1)S(1)} %broadcast_compare_fusion.2, bf16[4,88,3072]{2,1,0:T(8,128)(2,1)} %get-tuple-element.190, bf16[4,88,1024]{2,1,0:T(8,128)(2,1)S(1)} %get-tuple-element.189, s32[]{:T(128)S(6)} %select_n.147), kind=kOutput, calls=%fused_computation.126.clone.1 | convolution fusion | flops 1132465152 | bytes 29270020 | tf_op jit(solution)/shard_map/while/body/eval_jaxpr/sub | solution.py:119
  112.7 15.1 %fusion.90 = bf16[2,512,1408]{2,1,0:T(8,128)(2,1)} fusion(bf16[2,512,1408]{2,1,0:T(8,128)(2,1)} %get-tuple-element.173, s32[]{:T(128)} %get-tuple-element.172, bf16[4,88,1408]{2,1,0:T(8,128)(2,1)} %get-tuple-element.192, bf16[4,88,3072]{2,1,0:T(8,128)(2,1)} %get-tuple-element.191, f32[4,512,3072]{2,1,0:T(8,128)} %get-tuple-element.158, ...), kind=kOutput, calls=%fused_computation.13.clone.1 | convolution fusion | flops 1627570176 | bytes 31212032 | tf_op jit(solution)/shard_map/while/body/eval_jaxpr/hcq,hcd->qd/dot_general | solution.py:124
  131.5 15.8 %fusion.89 = (f32[4,512]{1,0:T(4,128)S(1)}, f32[4,512,3072]{2,1,0:T(8,128)}) fusion(pred[512,3072]{1,0:T(8,128)(4,1)S(1)} %broadcast_compare_fusion.2, bf16[4,88,3072]{2,1,0:T(8,128)(2,1)} %get-tuple-element.190, bf16[4,88,1024]{2,1,0:T(8,128)(2,1)S(1)} %get-tuple-element.189, s32[]{:T(128)S(6)} %select_n.147), kind=kOutput, calls=%fused_computation.126.clone.1 | convolution fusion | flops 1132465152 | bytes 29270020 | tf_op jit(solution)/shard_map/while/body/eval_jaxpr/sub | solution.py:119
  147.3 15.0 %fusion.90 = bf16[2,512,1408]{2,1,0:T(8,128)(2,1)} fusion(bf16[2,512,1408]{2,1,0:T(8,128)(2,1)} %get-tuple-element.173, s32[]{:T(128)} %get-tuple-element.172, bf16[4,88,1408]{2,1,0:T(8,128)(2,1)} %get-tuple-element.192, bf16[4,88,3072]{2,1,0:T(8,128)(2,1)} %get-tuple-element.191, f32[4,512,3072]{2,1,0:T(8,128)} %get-tuple-element.158, ...), kind=kOutput, calls=%fused_computation.13.clone.1 | convolution fusion | flops 1627570176 | bytes 31212032 | tf_op jit(solution)/shard_map/while/body/eval_jaxpr/hcq,hcd->qd/dot_general | solution.py:124
  163.9 1.6 scatter_custom_fusion
  166.1 6.8 %all-to-all-start = ((s32[8,64,1]{1,2,0:T(1,128)}), s32[8,64,1]{1,2,0:T(1,128)S(1)}, u32[]{:S(2)}, u32[]{:S(2)}) async-start(s32[8,64,1]{1,2,0:T(1,128)} %bitcast.7), calls=%async_computation | async-start | bytes 8192 | tf_op jit(solution)/shard_map/all_to_all | solution.py:149
  172.9 55.9 %all-reduce.2.cloned.1.call-done = bf16[1024,1408]{1,0:T(8,128)(2,1)} async-done(((bf16[1024,1408]{1,0:T(8,128)(2,1)}), bf16[1024,1408]{1,0:T(8,128)(2,1)}) %all-reduce.2.cloned.1.call-update) | async-done | bytes 2883600 | tf_op jit(solution)/shard_map/psum | solution.py:128
  228.9 4.1 %fusion.30 = bf16[1024,1408]{1,0:T(8,128)(2,1)} fusion(bf16[1024,1408]{1,0:T(8,128)(2,1)S(1)} %copy-done.3, bf16[1024,1408]{1,0:T(8,128)(2,1)} %all-reduce.2.cloned.1.call-done), kind=kLoop, calls=%fused_computation.34 | loop fusion | flops 5767168 | bytes 8650752 | tf_op jit(solution)/shard_map/convert_element_type | solution.py:129
  233.0 5.6 %reshape.244 = bf16[256,5632]{1,0:T(8,128)(2,1)} reshape(bf16[1024,1408]{1,0:T(8,128)(2,1)} %fusion.30) | data formatting | bytes 5767168 | tf_op jit(solution)/shard_map/reshape | solution.py:130
  238.6 5.3 %convolution_convert_fusion = bf16[256,512]{1,0:T(8,128)(2,1)S(1)} fusion(bf16[256,5632]{1,0:T(8,128)(2,1)} %reshape.244, bf16[5632,512]{1,0:T(8,128)(2,1)} %param.23), kind=kOutput, calls=%fused_computation.47 | convolution fusion | flops 1476526080 | bytes 8912896 | tf_op jit(solution)/shard_map/dot_general | solution.py:131
  243.9 2.3 scatter_custom_fusion.1
  246.2 5.5 %all-to-all-start.1 = ((bf16[8,64,512]{2,1,0:T(8,128)(2,1)}), bf16[8,64,512]{2,1,0:T(8,128)(2,1)S(1)}, u32[]{:S(2)}, u32[]{:S(2)}) async-start(bf16[8,64,512]{2,1,0:T(8,128)(2,1)} %bitcast.24), calls=%async_computation.1 | async-start | bytes 1048576 | tf_op jit(solution)/shard_map/all_to_all | solution.py:148
  253.0 13.1 %all-to-all-done.1 = bf16[8,64,512]{2,1,0:T(8,128)(2,1)S(1)} async-done(((bf16[8,64,512]{2,1,0:T(8,128)(2,1)}), bf16[8,64,512]{2,1,0:T(8,128)(2,1)S(1)}, u32[]{:S(2)}, u32[]{:S(2)}) %all-to-all-start.1) | async-done | bytes 524320 | tf_op jit(solution)/shard_map/all_to_all | solution.py:148
  266.1 3.0 %scatter_custom_fusion.2 = bf16[256,512]{1,0:T(8,128)(2,1)} fusion(s32[512]{0:T(512)S(1)} %bitcast.81, bf16[512,512]{1,0:T(8,128)(2,1)S(1)} %bitcast.79, bf16[]{:T(256)} %constant.105.clone.1), kind=kCustom, calls=%fused_computation.64 | custom fusion | bytes 262146 | tf_op jit(solution)/shard_map/scatter | solution.py:151
  (67 shorter events, 15.7 us)
Async XLA Ops:
  6.5 3.7 %copy-start = (bf16[3,352,1408]{2,1,0:T(8,128)(2,1)S(1)}, bf16[3,352,1408]{2,1,0:T(8,128)(2,1)}, u32[]{:S(2)}) copy-start(bf16[3,352,1408]{2,1,0:T(8,128)(2,1)} %param.21) | copy-start | bytes 8921092
  6.5 222.3 %all-reduce.2.cloned.1.call-start = ((), (), s32[]{:S(2)}) async-start(), calls=%async_computation.2 | async-start | bytes 5767168 | tf_op jit(solution)/shard_map/psum | solution.py:128
  6.5 2.8 %copy-start.2 = (bf16[1024,1408]{1,0:T(8,128)(2,1)S(1)}, bf16[1024,1408]{1,0:T(8,128)(2,1)}, u32[]{:S(2)}) copy-start(bf16[1024,1408]{1,0:T(8,128)(2,1)} %param.13) | copy-start | bytes 8650756
  6.6 3.7 %copy-start.9 = (f32[1408]{0:T(1024)S(1)}, f32[1408]{0:T(1024)}, u32[]{:S(2)}) copy-start(f32[1408]{0:T(1024)} %param.20) | copy-start | bytes 16900
  6.6 3.7 %copy-start.10 = (f32[1408]{0:T(1024)S(1)}, f32[1408]{0:T(1024)}, u32[]{:S(2)}) copy-start(f32[1408]{0:T(1024)} %param.19) | copy-start | bytes 16900
  14.1 1.5 copy-start.8
  14.1 2.1 copy-start.5
  14.1 2.8 %copy-start.7 = (s32[1024]{0:T(1024)S(1)}, s32[1024]{0:T(1024)}, u32[]{:S(2)}) copy-start(s32[1024]{0:T(1024)} %param.15) | copy-start | bytes 12292
  21.8 66.9 %collective-permute-start = (bf16[2,4,88,1024]{3,2,1,0:T(8,128)(2,1)}, bf16[2,4,88,1024]{3,2,1,0:T(8,128)(2,1)}, u32[]{:S(2)}, u32[]{:S(2)}) collective-permute-start(bf16[2,4,88,1024]{3,2,1,0:T(8,128)(2,1)} %pad_maximum_fusion.1), channel_id=1, source_target_pairs={{0,4},{4,8},{8,12},{12,16},{16,20},{20,24},{24,28},{1,5},{5,9},{9,... | collective-permute-start | bytes 4325384 | tf_op jit(solution)/shard_map/ppermute | solution.py:16
  27.7 60.9 %collective-permute-start.1 = (bf16[2,4,88,1024]{3,2,1,0:T(8,128)(2,1)}, bf16[2,4,88,1024]{3,2,1,0:T(8,128)(2,1)}, u32[]{:S(2)}, u32[]{:S(2)}) collective-permute-start(bf16[2,4,88,1024]{3,2,1,0:T(8,128)(2,1)} %pad_maximum_fusion.1), channel_id=1, source_target_pairs={{4,0},{8,4},{12,8},{16,12},{20,16},{24,20},{28,24},{5,1},{9,5},{13... | collective-permute-start | bytes 4325384 | tf_op jit(solution)/shard_map/ppermute | solution.py:17
  90.6 2.5 copy-start.4
  162.3 0.7 copy-start.6
  162.3 66.6 %copy-start.3 = (bf16[1024,1408]{1,0:T(8,128)(2,1)S(1)}, bf16[1024,1408]{1,0:T(8,128)(2,1)}, u32[]{:S(2)}) copy-start(bf16[1024,1408]{1,0:T(8,128)(2,1)} %param.13) | copy-start | bytes 8650756
  166.1 80.1 %all-to-all-start = ((s32[8,64,1]{1,2,0:T(1,128)}), s32[8,64,1]{1,2,0:T(1,128)S(1)}, u32[]{:S(2)}, u32[]{:S(2)}) async-start(s32[8,64,1]{1,2,0:T(1,128)} %bitcast.7), calls=%async_computation | async-start | bytes 8192 | tf_op jit(solution)/shard_map/all_to_all | solution.py:149
  238.6 30.5 %copy-start.1 = (bf16[3,352,1408]{2,1,0:T(8,128)(2,1)S(1)}, bf16[3,352,1408]{2,1,0:T(8,128)(2,1)}, u32[]{:S(2)}) copy-start(bf16[3,352,1408]{2,1,0:T(8,128)(2,1)} %param.21) | copy-start | bytes 8921092
  246.2 19.9 %all-to-all-start.1 = ((bf16[8,64,512]{2,1,0:T(8,128)(2,1)}), bf16[8,64,512]{2,1,0:T(8,128)(2,1)S(1)}, u32[]{:S(2)}, u32[]{:S(2)}) async-start(bf16[8,64,512]{2,1,0:T(8,128)(2,1)} %bitcast.24), calls=%async_computation.1 | async-start | bytes 1048576 | tf_op jit(solution)/shard_map/all_to_all | solution.py:148
Sparse Core Ops, SparseCore 0:
  162.4 66.3 all-reduce.1
where the time goes:
time: 277 us; the launch traced here: 276 us
  waiting for transfers between devices  125 us (45%)
  matrix products  70.8 us (26%)
  local copies, waits for them, and re-layouts  21.9 us (8%)
  other arithmetic  20.5 us (7%)
  starting transfers between devices  19.5 us (7%)
  between operations  14.3 us (5%)
  loops' own time  4.17 us (2%)
    psum x1, waiting for transfers between devices, on_device(): lax.psum(partial_value.astype(jnp.bfloat16), 'tp').astype(jnp.float32)  55.9 us
    ppermute x1, waiting for transfers between devices, extended(): before = lax.ppermute(last, axis, up)  55.8 us
    sub x2, matrix products, attend_block(): weights = jnp.exp(scores - largest)  31.7 us
    dot_general x2, matrix products, attend_block(): jnp.einsum('hcq,hcd->qd', heads_out, w_heads, preferred_element_type=jnp....  30.1 us
    all_to_all x1, waiting for transfers between devices, on_device(): lax.all_to_all(send_rows, 'req', split_axis=0, concat_axis=0, tiled=True)  13.1 us
    all_to_all x1, starting transfers between devices, on_device(): lax.all_to_all(send_dest, 'req', split_axis=0, concat_axis=0, tiled=True)  6.78 us
    ppermute x1, starting transfers between devices, extended(): before = lax.ppermute(last, axis, up)  5.95 us
    reshape x1, local copies, waits for them, and re-layouts, on_device(): merged = mixed_rows.reshape(tok_count // 4, 4 * feat_width)  5.62 us
  transfers between devices with their start and end apart: 5, of which 3 were waited for; matrix products, arithmetic and copies ran while one was open for 9% of the time, Pallas kernels for 0%

commit v1 on v0

v1 whole, which is shorter than its diff:
```python
import jax
import jax.numpy as jnp
from jax import lax
from jax.experimental import pallas as pl
from jax.experimental.pallas import tpu as pltpu
from jax.sharding import PartitionSpec as P

HD = 88


def layer_norm(inputs, scale_vec, shift_vec):
    widened = inputs.astype(jnp.float32)
    centred = widened - jnp.mean(widened, axis=-1, keepdims=True)
    variance = jnp.mean(centred * centred, axis=-1, keepdims=True)
    return (centred * lax.rsqrt(variance + 1e-06) * scale_vec + shift_vec).astype(jnp.bfloat16)


def grid_positions(seg_row, side_row, first_offset):
    row_len = seg_row.shape[0]
    tok_index = jnp.arange(row_len, dtype=jnp.int32)
    boundary = jnp.concatenate([jnp.ones((1,), dtype=bool), seg_row[1:] != seg_row[:-1]])
    seg_start = lax.cummax(jnp.where(boundary, tok_index, 0), axis=0)
    offset = tok_index - seg_start + jnp.where(seg_row == 0, first_offset, 0)
    half_side = side_row // 2
    window = offset // 4
    corner = offset % 4
    return (2 * (window // half_side) + corner // 2, 2 * (window % half_side) + corner % 2)


def rotate_pairs(channels, angles, axis_pos):
    quarter = channels.shape[axis_pos] // 2
    first_half = lax.slice_in_dim(channels, 0, quarter, axis=axis_pos)
    second_half = lax.slice_in_dim(channels, quarter, 2 * quarter, axis=axis_pos)
    cosine = jnp.cos(angles)
    sine_tab = jnp.sin(angles)
    return jnp.concatenate(
        [
            first_half * cosine - second_half * sine_tab,
            second_half * cosine + first_half * sine_tab,
        ],
        axis=axis_pos,
    )


def apply_rope(channels, row_angles, col_angles, axis_pos):
    half_width = channels.shape[axis_pos] // 2
    row_part = rotate_pairs(
        lax.slice_in_dim(channels, 0, half_width, axis=axis_pos), row_angles, axis_pos
    )
    col_part = rotate_pairs(
        lax.slice_in_dim(channels, half_width, 2 * half_width, axis=axis_pos), col_angles, axis_pos
    )
    return jnp.concatenate([row_part, col_part], axis=axis_pos)


def attend_tile(q_tile, k_ref, v_ref, kt, tile, allowed, state):
    largest, total, acc = state
    keys = k_ref[0, :, pl.ds(kt * tile, tile)]
    vals = v_ref[0, :, pl.ds(kt * tile, tile)]
    scores = lax.dot_general(
        keys, q_tile, (((0,), (0,)), ((), ())), preferred_element_type=jnp.float32
    )
    scores = jnp.where(allowed, scores, -1e30)
    larger = jnp.maximum(largest, jnp.max(scores, axis=0, keepdims=True))
    weights = jnp.exp2(scores - larger)
    decay = jnp.exp2(largest - larger)
    total = total * decay + jnp.sum(weights, axis=0, keepdims=True)
    acc = acc * decay + jnp.dot(
        vals, weights.astype(jnp.bfloat16), preferred_element_type=jnp.float32
    )
    return larger, total, acc


def own_kernel(tile, seg_s, q_ref, k_ref, v_ref, segq_ref, segk_ref, acc_ref, stat_ref):
    qt = pl.program_id(1)
    tiles = k_ref.shape[2] // tile
    q_tile = q_ref[0]
    q_lo, q_hi = (seg_s[qt * tile], seg_s[qt * tile + tile - 1])
    seg_q = segq_ref[...]
    stat_ref[0, 0:1, :] = jnp.full((1, tile), -1e30, jnp.float32)
    stat_ref[0, 1:2, :] = jnp.zeros((1, tile), jnp.float32)
    acc_ref[...] = jnp.zeros_like(acc_ref)
    for kt in range(tiles):
        k_lo, k_hi = (seg_s[kt * tile], seg_s[kt * tile + tile - 1])

        @pl.when((k_lo <= q_hi) & (q_lo <= k_hi))
        def _(kt=kt):
            allowed = segk_ref[kt * tile : (kt + 1) * tile, :] == seg_q
            state = (stat_ref[0, 0:1, :], stat_ref[0, 1:2, :], acc_ref[0])
            largest, total, acc = attend_tile(q_tile, k_ref, v_ref, kt, tile, allowed, state)
            stat_ref[0, 0:1, :] = largest
            stat_ref[0, 1:2, :] = total
            acc_ref[0] = acc


def near_kernel(
    tile, seg_s, plan_s, q_ref, kb_ref, vb_ref, ka_ref, va_ref, segq_ref, acc0_ref, stat0_ref,
    out_ref, stat_ref, acc_ref,
):
    qt = pl.program_id(1)
    length = kb_ref.shape[2]
    tiles = length // tile
    q_tile = q_ref[0]
    q_lo, q_hi, last = (seg_s[qt * tile], seg_s[qt * tile + tile - 1], seg_s[length - 1])
    from_before, from_after = (plan_s[0, 0], plan_s[0, 1])
    seg_q = segq_ref[...]
    stat_ref[...] = stat0_ref[0]
    acc_ref[...] = acc0_ref[0]

    def step(k_ref, v_ref, kt, allowed):
        state = (stat_ref[0:1, :], stat_ref[1:2, :], acc_ref[...])
        largest, total, acc = attend_tile(q_tile, k_ref, v_ref, kt, tile, allowed, state)
        stat_ref[0:1, :] = largest
        stat_ref[1:2, :] = total
        acc_ref[...] = acc

    for kt in range(tiles):
        rows = lax.broadcasted_iota(jnp.int32, (tile, tile), 0) + kt * tile

        @pl.when((q_lo == 0) & ((kt + 1) * tile > length - from_before))
        def _(kt=kt, rows=rows):
            step(kb_ref, vb_ref, kt, (rows >= length - from_before) & (seg_q == 0))

        @pl.when((q_hi == last) & (kt * tile < from_after))
        def _(kt=kt, rows=rows):
            step(ka_ref, va_ref, kt, (rows < from_after) & (seg_q == last))

    out_ref[0] = (acc_ref[...] / stat_ref[1:2, :]).astype(out_ref.dtype)


def attend_own(queries, keys, values, segment_ids, tile):
    heads, width, length = queries.shape
    whole = pl.BlockSpec((1, width, length), lambda h, t, *_: (h, 0, 0))
    tiled = pl.BlockSpec((1, width, tile), lambda h, t, *_: (h, 0, t))
    return pl.pallas_call(
        lambda *refs: own_kernel(tile, *refs),
        out_shape=(
            jax.ShapeDtypeStruct((heads, width, length), jnp.float32),
            jax.ShapeDtypeStruct((heads, 8, length), jnp.float32),
        ),
        grid_spec=pltpu.PrefetchScalarGridSpec(
            num_scalar_prefetch=1,
            grid=(heads, length // tile),
            in_specs=[
                tiled,
                whole,
                whole,
                pl.BlockSpec((1, tile), lambda h, t, *_: (0, t)),
                pl.BlockSpec((length, 1), lambda h, t, *_: (0, 0)),
            ],
            out_specs=(tiled, pl.BlockSpec((1, 8, tile), lambda h, t, *_: (h, 0, t))),
        ),
        compiler_params=pltpu.CompilerParams(vmem_limit_bytes=32 * 2**20),
        cost_estimate=pl.CostEstimate(
            flops=4 * heads * length * length * width,
            bytes_accessed=4 * heads * length * width * 2,
            transcendentals=heads * length * length,
        ),
        name="own_attention",
    )(segment_ids, queries, keys, values, segment_ids[None, :], segment_ids[:, None])


def attend_near(queries, before, after, segment_ids, split_plan, acc, stat, tile):
    heads, width, length = queries.shape
    whole = pl.BlockSpec((1, width, length), lambda h, t, *_: (h, 0, 0))
    tiled = pl.BlockSpec((1, width, tile), lambda h, t, *_: (h, 0, t))
    return pl.pallas_call(
        lambda *refs: near_kernel(tile, *refs),
        out_shape=jax.ShapeDtypeStruct((heads, width, length), jnp.bfloat16),
        grid_spec=pltpu.PrefetchScalarGridSpec(
            num_scalar_prefetch=2,
            grid=(heads, length // tile),
            in_specs=[
                tiled,
                whole,
                whole,
                whole,
                whole,
                pl.BlockSpec((1, tile), lambda h, t, *_: (0, t)),
                tiled,
                pl.BlockSpec((1, 8, tile), lambda h, t, *_: (h, 0, t)),
            ],
            out_specs=tiled,
            scratch_shapes=[
                pltpu.VMEM((8, tile), jnp.float32),
                pltpu.VMEM((width, tile), jnp.float32),
            ],
        ),
        compiler_params=pltpu.CompilerParams(vmem_limit_bytes=32 * 2**20),
        cost_estimate=pl.CostEstimate(
            flops=4 * heads * length * length * width,
            bytes_accessed=6 * heads * length * width * 2,
            transcendentals=heads * length * length,
        ),
        name="near_attention",
    )(
        segment_ids, split_plan, queries, before[0], before[1], after[0], after[1],
        segment_ids[None, :], acc, stat,
    )


def mix_kernel(ho_ref, wout_ref, patch_ref, wproj_ref, out_ref, mixed_ref):
    length, width = patch_ref.shape
    block = 256

    def mix(i, carry):
        rows = pl.ds(pl.multiple_of(i * block, block), block)
        total = lax.dot_general(
            ho_ref[:, rows], wout_ref[...], (((0,), (0,)), ((), ())),
            preferred_element_type=jnp.float32,
        )
        total = total + patch_ref[rows, :].astype(jnp.float32)
        for g in range(width // 128):
            mixed_ref[g, rows, :] = total[:, g * 128 : (g + 1) * 128]
        return carry

    lax.fori_loop(0, length // block, mix, 0)
    total = jnp.zeros(out_ref.shape, jnp.float32)
    for corner in range(4):
        part = jnp.concatenate(
            [
                mixed_ref[g, pl.ds(corner, length // 4, stride=4), :].astype(jnp.bfloat16)
                for g in range(width // 128)
            ],
            axis=1,
        )
        total += jnp.dot(
            part,
            wproj_ref[corner * width : (corner + 1) * width, :],
            preferred_element_type=jnp.float32,
        )
    out_ref[...] = total.astype(out_ref.dtype)


def mix_and_project(heads_out, w_out, patches, w_proj):
    length, width = patches.shape
    vmem = pl.BlockSpec(memory_space=pltpu.VMEM)
    return pl.pallas_call(
        mix_kernel,
        out_shape=jax.ShapeDtypeStruct((length // 4, w_proj.shape[1]), jnp.bfloat16),
        in_specs=[vmem] * 4,
        out_specs=vmem,
        scratch_shapes=[pltpu.VMEM((width // 128, length, 128), jnp.float32)],
        compiler_params=pltpu.CompilerParams(vmem_limit_bytes=48 * 2**20),
        name="mix_and_project",
    )(heads_out, w_out, patches, w_proj)


def on_device(
    patches,
    segment_ids,
    grid_sides,
    split_plan,
    owner_dev,
    dest_row,
    ln_gain,
    ln_bias,
    w_qkv,
    w_out,
    w_proj,
):
    tok_count = patches.shape[0]
    local_heads = w_qkv.shape[1] // HD
    tile = min(256, tok_count)
    w_out_all = lax.all_gather(w_out, "tp", axis=0, tiled=True)
    normed = layer_norm(patches, ln_gain, ln_bias)
    grid_row, grid_col = grid_positions(segment_ids, grid_sides, split_plan[0, 0])
    quarter = HD // 4
    frequency = 10000.0 ** (-jnp.arange(quarter, dtype=jnp.float32) / quarter)
    row_angles = frequency[:, None] * grid_row.astype(jnp.float32)[None, :]
    col_angles = frequency[:, None] * grid_col.astype(jnp.float32)[None, :]
    mixed_kv = jnp.einsum("td,kcd->kct", normed, w_qkv[1:], preferred_element_type=jnp.float32)
    shaped = mixed_kv.reshape(2, local_heads, HD, tok_count)
    keys = apply_rope(shaped[0], row_angles, col_angles, 1).astype(jnp.bfloat16)
    values = shaped[1].astype(jnp.bfloat16)
    count = lax.axis_size("req")
    up = [(i, i + 1) for i in range(count - 1)]
    down = [(j, i) for i, j in up]
    before = [lax.ppermute(part, "req", up) for part in (keys, values)]
    after = [lax.ppermute(part, "req", down) for part in (keys, values)]
    mixed_q = jnp.einsum("td,cd->ct", normed, w_qkv[0], preferred_element_type=jnp.float32)
    mixed_q = mixed_q.reshape(local_heads, HD, tok_count)
    scale = HD ** (-0.5) * 1.4426950408889634
    queries = (apply_rope(mixed_q, row_angles, col_angles, 1) * scale).astype(jnp.bfloat16)
    acc, stat = attend_own(queries, keys, values, segment_ids, tile)
    heads_out = attend_near(queries, before, after, segment_ids, split_plan, acc, stat, tile)
    heads_all = lax.all_gather(
        heads_out.reshape(local_heads * HD, tok_count), "tp", axis=0, tiled=True
    )
    projected = mix_and_project(heads_all, w_out_all, patches, w_proj)
    per_owner = owner_dev.shape[0]
    peer_count = lax.axis_size("req")
    owner_slots = 2 * per_owner // peer_count
    matches = (owner_dev[:, None] == jnp.arange(peer_count, dtype=jnp.int32)[None, :]).astype(
        jnp.int32
    )
    arrival = jnp.sum(jnp.cumsum(matches, axis=0) * matches, axis=1) - 1
    send_slot = owner_dev * owner_slots + arrival
    slots = jnp.arange(peer_count * owner_slots, dtype=jnp.int32)
    hit = slots[:, None] == send_slot[None, :]
    send_dest = jnp.sum(jnp.where(hit, dest_row[None, :] + 1, 0), axis=1) - 1
    got_dest = lax.all_to_all(send_dest, "req", split_axis=0, concat_axis=0, tiled=True)
    place = (jnp.arange(per_owner, dtype=jnp.int32)[:, None] == got_dest[None, :]).astype(
        jnp.bfloat16
    )
    send_rows = jnp.dot(
        hit.astype(jnp.bfloat16), projected, preferred_element_type=jnp.float32
    ).astype(jnp.bfloat16)
    got_rows = lax.all_to_all(send_rows, "req", split_axis=0, concat_axis=0, tiled=True)
    return jnp.dot(place, got_rows, preferred_element_type=jnp.float32).astype(jnp.bfloat16)


def solution(mesh):
    placed = (
        P("req", None),
        P("req"),
        P("req"),
        P("req", None),
        P("req"),
        P("req"),
        P(),
        P(),
        P(None, "tp", None),
        P("tp", None),
        P(None, "tp"),
    )
    return jax.shard_map(
        on_device, mesh=mesh, in_specs=placed, out_specs=P("req", "tp"), check_vma=False
    )
```

time: 277 us -> 211 us (0.76)
  matrix products: 70.8 us -> 10.1 us
  Pallas kernels: 0 us -> 54.5 us
  waiting for transfers between devices: 125 us -> 84.8 us
  local copies, waits for them, and re-layouts: 21.9 us -> 6.26 us
  starting transfers between devices: 19.5 us -> 29.7 us
  other arithmetic: 20.5 us -> 10.4 us
  loops' own time: 4.17 us -> 0 us
    psum x1 -> x0, waiting for transfers between devices: 55.9 us -> none  [on_device(): lax.psum(partial_value.astype(jnp.bfloat16), 'tp').astype(jnp.float32)]
    all_gather x0 -> x2, waiting for transfers between devices: none -> 54.9 us  [the longest x1 34.8 us: on_device(): w_out_all = lax.all_gather(w_out, 'tp', axis=0, tiled=True)]
    pallas_call x0 -> x3, Pallas kernels: none -> 54.5 us  [the longest x1 30.6 us: attend_own(): pl.pallas_call(lambda *refs: own_kernel(tile, *refs), out_shape=(jax.Shap...]
    ppermute x2 -> x4, waiting for transfers between devices: 55.8 us -> 15.6 us  [the longest x2 15.5 us: on_device(): before = [lax.ppermute(part, 'req', up) for part in (keys, values)]]
    sub x2 -> x0, matrix products: 31.7 us -> none  [attend_block(): weights = jnp.exp(scores - largest)]
    dot_general x4, matrix products: 39.1 us -> 10.1 us  [the longest x1 4.14 us: on_device(): jnp.einsum('td,kcd->kct', normed, w_qkv[1:], preferred_element_type=jnp.f...]
    scatter x3 -> x0, local copies, waits for them, and re-layouts: 6.89 us -> none  [the longest x1 3.02 us: on_device(): jnp.zeros((per_owner, out_cols), jnp.bfloat16).at[got_dest]]
    ppermute x2 -> x4, starting transfers between devices: 7.23 us -> 13.7 us  [the longest x2 11.1 us: on_device(): before = [lax.ppermute(part, 'req', up) for part in (keys, values)]]
  transfers between devices with their start and end apart: 5 -> 8, of which waited for: 3 -> 5; matrix products, arithmetic and copies ran while one was open for 9% -> 5% of each run, Pallas kernels for 0% -> 20%
where the time goes in v1:
time: 211 us; the launch traced here: 209 us
  waiting for transfers between devices  84.8 us (40%)
  Pallas kernels  54.5 us (26%)
  starting transfers between devices  29.7 us (14%)
  between operations  13.7 us (6%)
  other arithmetic  10.4 us (5%)
  matrix products  10.1 us (5%)
  local copies, waits for them, and re-layouts  6.26 us (3%)
    all_gather x1, waiting for transfers between devices, on_device(): w_out_all = lax.all_gather(w_out, 'tp', axis=0, tiled=True)  34.8 us
    pallas_call x1, Pallas kernels, attend_own(): pl.pallas_call(lambda *refs: own_kernel(tile, *refs), out_shape=(jax.Shap...  30.6 us
    all_gather x1, waiting for transfers between devices, on_device(): lax.all_gather(heads_out.reshape(local_heads * HD, tok_count), 'tp', axis...  20.1 us
    ppermute x2, waiting for transfers between devices, on_device(): before = [lax.ppermute(part, 'req', up) for part in (keys, values)]  15.5 us
    all_to_all x1, waiting for transfers between devices, on_device(): lax.all_to_all(send_rows, 'req', split_axis=0, concat_axis=0, tiled=True)  13.6 us
    pallas_call x1, Pallas kernels, attend_near(): pl.pallas_call(lambda *refs: near_kernel(tile, *refs), out_shape=jax.Shap...  12.7 us
    pallas_call x1, Pallas kernels, mix_and_project(): pl.pallas_call(mix_kernel, out_shape=jax.ShapeDtypeStruct((length // 4, w...  11.3 us
    ppermute x2, starting transfers between devices, on_device(): before = [lax.ppermute(part, 'req', up) for part in (keys, values)]  11.1 us
  transfers between devices with their start and end apart: 8, of which 5 were waited for; matrix products, arithmetic and copies ran while one was open for 5% of the time, Pallas kernels for 20%

profile of v1, /device:TPU:0, one launch (start us, length us, event | category | flops | bytes accessed | tf_op | source)
XLA Modules:
  0.0 209.5 jit_solution(11544278671474518322)
XLA Ops:
  6.5 0.9 slice_compare_fusion
  8.1 2.3 %convert_reduce_fusion = f32[1024]{0:T(1024)S(1)} fusion(bf16[1024,1408]{1,0:T(8,128)(2,1)} %patch_ref.1), kind=kLoop, calls=%fused_computation.1 | loop fusion | flops 2882560 | bytes 2887680 | tf_op jit(solution)/shard_map/reduce_sum | solution.py:13
  11.3 4.1 %fusion.9 = f32[2,352,1024]{2,1,0:T(8,128)S(1)} fusion(bf16[3,352,1408]{2,1,0:T(8,128)(2,1)} %param.19, bf16[1024,1408]{1,0:T(8,128)(2,1)S(1)} %copy-done, f32[1408]{0:T(1024)S(1)} %copy-done.11, f32[1408]{0:T(1024)S(1)} %copy-done.12, f32[1024]{0:T(1024)S(1)} %add_rsqrt_fusion, f32[1024]{0:T(1024)S(1)} %broadcast_multiply_fusion), kind=kOutput, calls=%fused_computation.11 | convolution fusion | flops 2038693888 | bytes 7769088 | tf_op jit(solution)/shard_map/td,kcd->kct/dot_general | solution.py:272
  17.5 1.1 pad_maximum_fusion.refs_2_
  18.6 5.7 %collective-permute-start = (bf16[4,88,1024]{2,1,0:T(8,128)(2,1)}, bf16[4,88,1024]{2,1,0:T(8,128)(2,1)}, u32[]{:S(2)}, u32[]{:S(2)}) collective-permute-start(bf16[4,88,1024]{2,1,0:T(8,128)(2,1)} %pad_maximum_fusion.refs_2_), channel_id=1, source_target_pairs={{0,4},{4,8},{8,12},{12,16},{16,20},{20,24},{24,28},{1,5},{5,9},{9,... | collective-permute-start | bytes 2162696 | tf_op jit(solution)/shard_map/ppermute | solution.py:279
  24.3 1.3 collective-permute-start.2
  25.6 1.0 slice.133
  26.6 5.4 %collective-permute-start.1 = (bf16[4,88,1024]{2,1,0:T(8,128)(2,1)}, bf16[4,88,1024]{2,1,0:T(8,128)(2,1)}, u32[]{:S(2)}, u32[]{:S(2)}) collective-permute-start(bf16[4,88,1024]{2,1,0:T(8,128)(2,1)} %bitcast.14.refs_3_), channel_id=1, source_target_pairs={{0,4},{4,8},{8,12},{12,16},{16,20},{20,24},{24,28},{1,5},{5,9},{9,... | collective-permute-start | bytes 2162696 | tf_op jit(solution)/shard_map/ppermute | solution.py:279
  32.0 1.3 collective-permute-start.3
  33.3 3.8 %fusion.15 = f32[1024,352]{0,1:T(8,128)} fusion(bf16[3,352,1408]{2,1,0:T(8,128)(2,1)} %param.19, bf16[1024,1408]{1,0:T(8,128)(2,1)S(1)} %copy-done, f32[1408]{0:T(1024)S(1)} %copy-done.11, f32[1408]{0:T(1024)S(1)} %copy-done.12, f32[1024]{0:T(1024)S(1)} %add_rsqrt_fusion, f32[1024]{0:T(1024)S(1)} %broadcast_multiply_fusion), kind=kOutput, calls=%fused_computation.17 | convolution fusion | flops 1023672320 | bytes 5336064 | tf_op jit(solution)/shard_map/td,cd->ct/dot_general | solution.py:281
  37.3 1.8 multiply_subtract_fusion.1
  39.3 30.6 %own_attention.1 = (f32[4,88,1024]{2,1,0:T(8,128)S(1)}, f32[4,8,1024]{2,1,0:T(8,128)S(1)}) custom-call(s32[1024]{0:T(1024)S(1)} %copy-done.3, bf16[4,88,1024]{2,1,0:T(8,128)(2,1)S(1)} %fusion.14.refs_1_.refs_2_, bf16[4,88,1024]{2,1,0:T(8,128)(2,1)} %pad_maximum_fusion.refs_2_, bf16[4,88,1024]{2,1,0:T(8,128)(2,1)} %bitcast.14.refs_3_, ...), custom_call_target="tpu_custom_call" | custom-call | flops 1476395008 | bytes 2883584 | tf_op jit(solution)/shard_map/own_attention/pallas_call | solution.py:135
  69.9 1.2 collective-permute-done.refs_3_
  71.2 14.3 %collective-permute-done.1.refs_4_ = bf16[4,88,1024]{2,1,0:T(8,128)(2,1)} collective-permute-done((bf16[4,88,1024]{2,1,0:T(8,128)(2,1)}, bf16[4,88,1024]{2,1,0:T(8,128)(2,1)}, u32[]{:S(2)}, u32[]{:S(2)}) %collective-permute-start.1) | collective-permute-done | bytes 720928 | tf_op jit(solution)/shard_map/ppermute | solution.py:279
  85.5 12.7 %near_attention.1 = bf16[4,88,1024]{2,1,0:T(8,128)(2,1)S(1)} custom-call(s32[1024]{0:T(1024)S(1)} %copy-done.3, s32[1,2]{1,0:T(1,128)S(1)} %copy-done.4, bf16[4,88,1024]{2,1,0:T(8,128)(2,1)S(1)} %fusion.14.refs_1_.refs_2_, bf16[4,88,1024]{2,1,0:T(8,128)(2,1)} %collective-permute-done.refs_3_, bf16[4,88,1024]{2,1,0:T(8,128)(2,1)} %collective-permute-done.1.refs_4_, ...), custom_call_target="tpu_custom_call" | custom-call | flops 1476395008 | bytes 4325376 | tf_op jit(solution)/shard_map/near_attention/pallas_call | solution.py:167
  101.6 10.5 %all-to-all-start = ((s32[8,64,1]{1,2,0:T(1,128)}), s32[8,64,1]{1,2,0:T(1,128)S(1)}, u32[]{:S(2)}, u32[]{:S(2)}) async-start(s32[8,64,1]{1,2,0:T(1,128)} %bitcast.3), calls=%async_computation | async-start | bytes 8192 | tf_op jit(solution)/shard_map/all_to_all | solution.py:302
  112.1 20.1 %all-gather.3.cloned.1.call-done.ho_ref = bf16[1408,1024]{1,0:T(8,128)(2,1)} async-done(((bf16[352,1024]{1,0:T(8,128)(2,1)}), bf16[1408,1024]{1,0:T(8,128)(2,1)}) %all-gather.3.cloned.1.call-update) | async-done | bytes 2883600 | tf_op jit(solution)/shard_map/all_gather | solution.py:287
  132.2 34.8 %all-gather.5.cloned.1.call-done.wout_ref = bf16[1408,1408]{1,0:T(8,128)(2,1)} async-done(((bf16[352,1408]{1,0:T(8,128)(2,1)}), bf16[1408,1408]{1,0:T(8,128)(2,1)}) %all-gather.5.cloned.1.call-update) | async-done | bytes 3964944 | tf_op jit(solution)/shard_map/all_gather | solution.py:265
  167.0 1.8 copy-done.1
  168.8 11.3 %mix_and_project.1 = bf16[256,512]{1,0:T(8,128)(2,1)S(1)} custom-call(bf16[1408,1024]{1,0:T(8,128)(2,1)S(1)} %copy-done.1, bf16[1408,1408]{1,0:T(8,128)(2,1)} %all-gather.5.cloned.1.call-done.wout_ref, bf16[1024,1408]{1,0:T(8,128)(2,1)S(1)} %copy-done, bf16[5632,512]{1,0:T(8,128)(2,1)} %wproj_ref.1), custom_call_target="tpu_custom_call" | custom-call | tf_op jit(solution)/shard_map/mix_and_project/pallas_call | solution.py:238
  180.1 1.1 convolution_convert_fusion
  181.2 5.5 %all-to-all-start.1 = ((bf16[8,64,512]{2,1,0:T(8,128)(2,1)}), bf16[8,64,512]{2,1,0:T(8,128)(2,1)S(1)}, u32[]{:S(2)}, u32[]{:S(2)}) async-start(bf16[8,64,512]{2,1,0:T(8,128)(2,1)} %bitcast.18), calls=%async_computation.1 | async-start | bytes 1048576 | tf_op jit(solution)/shard_map/all_to_all | solution.py:309
  188.0 13.6 %all-to-all-done.1 = bf16[8,64,512]{2,1,0:T(8,128)(2,1)S(1)} async-done(((bf16[8,64,512]{2,1,0:T(8,128)(2,1)}), bf16[8,64,512]{2,1,0:T(8,128)(2,1)S(1)}, u32[]{:S(2)}, u32[]{:S(2)}) %all-to-all-start.1) | async-done | bytes 524320 | tf_op jit(solution)/shard_map/all_to_all | solution.py:309
  201.6 1.0 convolution_convert_fusion.1
  (61 shorter events, 8.6 us)
Async XLA Ops:
  6.5 3.8 %copy-start = (bf16[1024,1408]{1,0:T(8,128)(2,1)S(1)}, bf16[1024,1408]{1,0:T(8,128)(2,1)}, u32[]{:S(2)}) copy-start(bf16[1024,1408]{1,0:T(8,128)(2,1)} %patch_ref.1) | copy-start | bytes 8650756
  6.5 125.7 %all-gather.3.cloned.1.call-start = ((), (), s32[]{:S(2)}) async-start(), calls=%async_computation.2 | async-start | bytes 3604480 | tf_op jit(solution)/shard_map/all_gather | solution.py:287
  8.1 3.2 %copy-start.11 = (f32[1408]{0:T(1024)S(1)}, f32[1408]{0:T(1024)}, u32[]{:S(2)}) copy-start(f32[1408]{0:T(1024)} %param.18) | copy-start | bytes 16900
  8.1 3.2 %copy-start.12 = (f32[1408]{0:T(1024)S(1)}, f32[1408]{0:T(1024)}, u32[]{:S(2)}) copy-start(f32[1408]{0:T(1024)} %param.17) | copy-start | bytes 16900
  15.4 0.7 copy-start.3
  15.5 0.7 copy-start.4
  15.5 0.7 copy-start.9
  17.2 9.4 %copy-start.5 = (f32[22,1024]{1,0:T(8,128)}, f32[22,1024]{1,0:T(8,128)S(1)}, u32[]{:S(2)}) copy-start(f32[22,1024]{1,0:T(8,128)S(1)} %get-tuple-element.24) | copy-start | bytes 270340
  17.2 9.4 %copy-start.6 = (f32[22,1024]{1,0:T(8,128)}, f32[22,1024]{1,0:T(8,128)S(1)}, u32[]{:S(2)}) copy-start(f32[22,1024]{1,0:T(8,128)S(1)} %get-tuple-element.27) | copy-start | bytes 270340
  17.2 14.8 %copy-start.7 = (f32[22,1024]{1,0:T(8,128)}, f32[22,1024]{1,0:T(8,128)S(1)}, u32[]{:S(2)}) copy-start(f32[22,1024]{1,0:T(8,128)S(1)} %get-tuple-element.28) | copy-start | bytes 270340
  18.6 52.6 %collective-permute-start = (bf16[4,88,1024]{2,1,0:T(8,128)(2,1)}, bf16[4,88,1024]{2,1,0:T(8,128)(2,1)}, u32[]{:S(2)}, u32[]{:S(2)}) collective-permute-start(bf16[4,88,1024]{2,1,0:T(8,128)(2,1)} %pad_maximum_fusion.refs_2_), channel_id=1, source_target_pairs={{0,4},{4,8},{8,12},{12,16},{16,20},{20,24},{24,28},{1,5},{5,9},{9,... | collective-permute-start | bytes 2162696 | tf_op jit(solution)/shard_map/ppermute | solution.py:279
  24.3 46.9 %collective-permute-start.2 = (bf16[4,88,1024]{2,1,0:T(8,128)(2,1)}, bf16[4,88,1024]{2,1,0:T(8,128)(2,1)}, u32[]{:S(2)}, u32[]{:S(2)}) collective-permute-start(bf16[4,88,1024]{2,1,0:T(8,128)(2,1)} %pad_maximum_fusion.refs_2_), channel_id=1, source_target_pairs={{4,0},{8,4},{12,8},{16,12},{20,16},{24,20},{28,24},{5,1},{9,5},{13... | collective-permute-start | bytes 2162696 | tf_op jit(solution)/shard_map/ppermute | solution.py:280
  26.6 58.9 %collective-permute-start.1 = (bf16[4,88,1024]{2,1,0:T(8,128)(2,1)}, bf16[4,88,1024]{2,1,0:T(8,128)(2,1)}, u32[]{:S(2)}, u32[]{:S(2)}) collective-permute-start(bf16[4,88,1024]{2,1,0:T(8,128)(2,1)} %bitcast.14.refs_3_), channel_id=1, source_target_pairs={{0,4},{4,8},{8,12},{12,16},{16,20},{20,24},{24,28},{1,5},{5,9},{9,... | collective-permute-start | bytes 2162696 | tf_op jit(solution)/shard_map/ppermute | solution.py:279
  32.0 53.5 %collective-permute-start.3 = (bf16[4,88,1024]{2,1,0:T(8,128)(2,1)}, bf16[4,88,1024]{2,1,0:T(8,128)(2,1)}, u32[]{:S(2)}, u32[]{:S(2)}) collective-permute-start(bf16[4,88,1024]{2,1,0:T(8,128)(2,1)} %bitcast.14.refs_3_), channel_id=1, source_target_pairs={{4,0},{8,4},{12,8},{16,12},{20,16},{24,20},{28,24},{5,1},{9,5},{13... | collective-permute-start | bytes 2162696 | tf_op jit(solution)/shard_map/ppermute | solution.py:280
  85.5 14.3 %copy-start.8 = (s32[256]{0:T(256)S(1)}, s32[256]{0:T(256)}, u32[]{:S(2)}) copy-start(s32[256]{0:T(256)} %param.15) | copy-start | bytes 3076
  85.5 15.3 %copy-start.10 = (s32[256]{0:T(256)S(1)}, s32[256]{0:T(256)}, u32[]{:S(2)}) copy-start(s32[256]{0:T(256)} %param.16) | copy-start | bytes 3076
  98.1 0.9 copy-start.2
  99.0 67.9 %all-gather.5.cloned.1.call-start = ((), (), s32[]{:S(2)}) async-start(), calls=%async_computation.3 | async-start | bytes 4956160 | tf_op jit(solution)/shard_map/all_gather | solution.py:265
  101.6 79.6 %all-to-all-start = ((s32[8,64,1]{1,2,0:T(1,128)}), s32[8,64,1]{1,2,0:T(1,128)S(1)}, u32[]{:S(2)}, u32[]{:S(2)}) async-start(s32[8,64,1]{1,2,0:T(1,128)} %bitcast.3), calls=%async_computation | async-start | bytes 8192 | tf_op jit(solution)/shard_map/all_to_all | solution.py:302
  167.0 1.8 copy-start.1
  181.2 20.4 %all-to-all-start.1 = ((bf16[8,64,512]{2,1,0:T(8,128)(2,1)}), bf16[8,64,512]{2,1,0:T(8,128)(2,1)S(1)}, u32[]{:S(2)}, u32[]{:S(2)}) async-start(bf16[8,64,512]{2,1,0:T(8,128)(2,1)} %bitcast.18), calls=%async_computation.1 | async-start | bytes 1048576 | tf_op jit(solution)/shard_map/all_to_all | solution.py:309
Sparse Core Ops, SparseCore 0:
  99.2 32.9 all-gather.2
  133.8 33.1 all-gather.4

commit v2 on v1

--- a/solution.py
+++ b/solution.py
@@ -53,10 +53,10 @@
     return jnp.concatenate([row_part, col_part], axis=axis_pos)
 
 
-def attend_tile(q_tile, k_ref, v_ref, kt, tile, allowed, state):
+def attend_tile(q_tile, k_ref, v_ref, head, kt, tile, allowed, state):
     largest, total, acc = state
-    keys = k_ref[0, :, pl.ds(kt * tile, tile)]
-    vals = v_ref[0, :, pl.ds(kt * tile, tile)]
+    keys = k_ref[head, :, pl.ds(kt * tile, tile)]
+    vals = v_ref[head, :, pl.ds(kt * tile, tile)]
     scores = lax.dot_general(
         keys, q_tile, (((0,), (0,)), ((), ())), preferred_element_type=jnp.float32
     )
@@ -72,13 +72,13 @@
 
 
 def own_kernel(tile, seg_s, q_ref, k_ref, v_ref, segq_ref, segk_ref, acc_ref, stat_ref):
-    qt = pl.program_id(1)
+    qt = pl.program_id(0)
+    heads = q_ref.shape[0]
     tiles = k_ref.shape[2] // tile
-    q_tile = q_ref[0]
     q_lo, q_hi = (seg_s[qt * tile], seg_s[qt * tile + tile - 1])
     seg_q = segq_ref[...]
-    stat_ref[0, 0:1, :] = jnp.full((1, tile), -1e30, jnp.float32)
-    stat_ref[0, 1:2, :] = jnp.zeros((1, tile), jnp.float32)
+    stat_ref[:, 0:1, :] = jnp.full((heads, 1, tile), -1e30, jnp.float32)
+    stat_ref[:, 1:8, :] = jnp.zeros((heads, 7, tile), jnp.float32)
     acc_ref[...] = jnp.zeros_like(acc_ref)
     for kt in range(tiles):
         k_lo, k_hi = (seg_s[kt * tile], seg_s[kt * tile + tile - 1])
@@ -86,52 +86,66 @@
         @pl.when((k_lo <= q_hi) & (q_lo <= k_hi))
         def _(kt=kt):
             allowed = segk_ref[kt * tile : (kt + 1) * tile, :] == seg_q
-            state = (stat_ref[0, 0:1, :], stat_ref[0, 1:2, :], acc_ref[0])
-            largest, total, acc = attend_tile(q_tile, k_ref, v_ref, kt, tile, allowed, state)
-            stat_ref[0, 0:1, :] = largest
-            stat_ref[0, 1:2, :] = total
-            acc_ref[0] = acc
+            states = [
+                attend_tile(
+                    q_ref[h], k_ref, v_ref, h, kt, tile, allowed,
+                    (stat_ref[h, 0:1, :], stat_ref[h, 1:2, :], acc_ref[h]),
+                )
+                for h in range(heads)
+            ]
+            for h, (largest, total, acc) in enumerate(states):
+                stat_ref[h, 0:1, :] = largest
+                stat_ref[h, 1:2, :] = total
+                acc_ref[h] = acc
 
 
 def near_kernel(
-    tile, seg_s, plan_s, q_ref, kb_ref, vb_ref, ka_ref, va_ref, segq_ref, acc0_ref, stat0_ref,
+    tile, seg_s, plan_s, q_ref, before_ref, after_ref, segq_ref, acc0_ref, stat0_ref,
     out_ref, stat_ref, acc_ref,
 ):
-    qt = pl.program_id(1)
-    length = kb_ref.shape[2]
+    qt = pl.program_id(0)
+    heads = q_ref.shape[0]
+    length = before_ref.shape[3]
     tiles = length // tile
-    q_tile = q_ref[0]
     q_lo, q_hi, last = (seg_s[qt * tile], seg_s[qt * tile + tile - 1], seg_s[length - 1])
     from_before, from_after = (plan_s[0, 0], plan_s[0, 1])
     seg_q = segq_ref[...]
-    stat_ref[...] = stat0_ref[0]
-    acc_ref[...] = acc0_ref[0]
-
-    def step(k_ref, v_ref, kt, allowed):
-        state = (stat_ref[0:1, :], stat_ref[1:2, :], acc_ref[...])
-        largest, total, acc = attend_tile(q_tile, k_ref, v_ref, kt, tile, allowed, state)
-        stat_ref[0:1, :] = largest
-        stat_ref[1:2, :] = total
-        acc_ref[...] = acc
+    stat_ref[...] = stat0_ref[...]
+    acc_ref[...] = acc0_ref[...]
+
+    def step(kv_ref, kt, allowed):
+        states = [
+            attend_tile(
+                q_ref[h], kv_ref.at[0], kv_ref.at[1], h, kt, tile, allowed,
+                (stat_ref[h, 0:1, :], stat_ref[h, 1:2, :], acc_ref[h]),
+            )
+            for h in range(heads)
+        ]
+        for h, (largest, total, acc) in enumerate(states):
+            stat_ref[h, 0:1, :] = largest
+            stat_ref[h, 1:2, :] = total
+            acc_ref[h] = acc
 
     for kt in range(tiles):
-        rows = lax.broadcasted_iota(jnp.int32, (tile, tile), 0) + kt * tile
 
         @pl.when((q_lo == 0) & ((kt + 1) * tile > length - from_before))
-        def _(kt=kt, rows=rows):
-            step(kb_ref, vb_ref, kt, (rows >= length - from_before) & (seg_q == 0))
+        def _(kt=kt):
+            rows = lax.broadcasted_iota(jnp.int32, (tile, tile), 0) + kt * tile
+            step(before_ref, kt, (rows >= length - from_before) & (seg_q == 0))
 
         @pl.when((q_hi == last) & (kt * tile < from_after))
-        def _(kt=kt, rows=rows):
-            step(ka_ref, va_ref, kt, (rows < from_after) & (seg_q == last))
-
-    out_ref[0] = (acc_ref[...] / stat_ref[1:2, :]).astype(out_ref.dtype)
+        def _(kt=kt):
+            rows = lax.broadcasted_iota(jnp.int32, (tile, tile), 0) + kt * tile
+            step(after_ref, kt, (rows < from_after) & (seg_q == last))
+
+    for h in range(heads):
+        out_ref[h] = (acc_ref[h] / stat_ref[h, 1:2, :]).astype(out_ref.dtype)
 
 
 def attend_own(queries, keys, values, segment_ids, tile):
     heads, width, length = queries.shape
-    whole = pl.BlockSpec((1, width, length), lambda h, t, *_: (h, 0, 0))
-    tiled = pl.BlockSpec((1, width, tile), lambda h, t, *_: (h, 0, t))
+    whole = pl.BlockSpec((heads, width, length), lambda t, *_: (0, 0, 0))
+    tiled = pl.BlockSpec((heads, width, tile), lambda t, *_: (0, 0, t))
     return pl.pallas_call(
         lambda *refs: own_kernel(tile, *refs),
         out_shape=(
@@ -140,15 +154,15 @@
         ),
         grid_spec=pltpu.PrefetchScalarGridSpec(
             num_scalar_prefetch=1,
-            grid=(heads, length // tile),
+            grid=(length // tile,),
             in_specs=[
                 tiled,
                 whole,
                 whole,
-                pl.BlockSpec((1, tile), lambda h, t, *_: (0, t)),
-                pl.BlockSpec((length, 1), lambda h, t, *_: (0, 0)),
+                pl.BlockSpec((1, tile), lambda t, *_: (0, t)),
+                pl.BlockSpec((length, 1), lambda t, *_: (0, 0)),
             ],
-            out_specs=(tiled, pl.BlockSpec((1, 8, tile), lambda h, t, *_: (h, 0, t))),
+            out_specs=(tiled, pl.BlockSpec((heads, 8, tile), lambda t, *_: (0, 0, t))),
         ),
         compiler_params=pltpu.CompilerParams(vmem_limit_bytes=32 * 2**20),
         cost_estimate=pl.CostEstimate(
@@ -160,30 +174,28 @@
     )(segment_ids, queries, keys, values, segment_ids[None, :], segment_ids[:, None])
 
 
-def attend_near(queries, before, after, segment_ids, split_plan, acc, stat, tile):
-    heads, width, length = queries.shape
-    whole = pl.BlockSpec((1, width, length), lambda h, t, *_: (h, 0, 0))
-    tiled = pl.BlockSpec((1, width, tile), lambda h, t, *_: (h, 0, t))
+def attend_near(queries, before, after, segment_ids, split_plan, acc, stat, tile, part):
+    _, heads, width, length = before.shape
+    whole = pl.BlockSpec((2, heads, width, length), lambda t, *_: (0, 0, 0, 0))
+    tiled = pl.BlockSpec((heads, width, tile), lambda t, *_: (part, 0, t))
     return pl.pallas_call(
         lambda *refs: near_kernel(tile, *refs),
         out_shape=jax.ShapeDtypeStruct((heads, width, length), jnp.bfloat16),
         grid_spec=pltpu.PrefetchScalarGridSpec(
             num_scalar_prefetch=2,
-            grid=(heads, length // tile),
+            grid=(length // tile,),
             in_specs=[
                 tiled,
                 whole,
                 whole,
-                whole,
-                whole,
-                pl.BlockSpec((1, tile), lambda h, t, *_: (0, t)),
+                pl.BlockSpec((1, tile), lambda t, *_: (0, t)),
                 tiled,
-                pl.BlockSpec((1, 8, tile), lambda h, t, *_: (h, 0, t)),
+                pl.BlockSpec((heads, 8, tile), lambda t, *_: (part, 0, t)),
             ],
-            out_specs=tiled,
+            out_specs=pl.BlockSpec((heads, width, tile), lambda t, *_: (0, 0, t)),
             scratch_shapes=[
-                pltpu.VMEM((8, tile), jnp.float32),
-                pltpu.VMEM((width, tile), jnp.float32),
+                pltpu.VMEM((heads, 8, tile), jnp.float32),
+                pltpu.VMEM((heads, width, tile), jnp.float32),
             ],
         ),
         compiler_params=pltpu.CompilerParams(vmem_limit_bytes=32 * 2**20),
@@ -194,22 +206,23 @@
         ),
         name="near_attention",
     )(
-        segment_ids, split_plan, queries, before[0], before[1], after[0], after[1],
+        segment_ids, split_plan, queries, before, after,
         segment_ids[None, :], acc, stat,
     )
 
 
-def mix_kernel(ho_ref, wout_ref, patch_ref, wproj_ref, out_ref, mixed_ref):
+def mix_kernel(ho_a_ref, ho_b_ref, wa_ref, wb_ref, patch_ref, wproj_ref, out_ref, mixed_ref):
     length, width = patch_ref.shape
     block = 256
 
     def mix(i, carry):
         rows = pl.ds(pl.multiple_of(i * block, block), block)
-        total = lax.dot_general(
-            ho_ref[:, rows], wout_ref[...], (((0,), (0,)), ((), ())),
-            preferred_element_type=jnp.float32,
-        )
-        total = total + patch_ref[rows, :].astype(jnp.float32)
+        total = patch_ref[rows, :].astype(jnp.float32)
+        for ho_ref, w_ref in ((ho_a_ref, wa_ref), (ho_b_ref, wb_ref)):
+            total = total + lax.dot_general(
+                ho_ref[:, rows], w_ref[...], (((0,), (0,)), ((), ())),
+                preferred_element_type=jnp.float32,
+            )
         for g in range(width // 128):
             mixed_ref[g, rows, :] = total[:, g * 128 : (g + 1) * 128]
         return carry
@@ -238,12 +251,12 @@
     return pl.pallas_call(
         mix_kernel,
         out_shape=jax.ShapeDtypeStruct((length // 4, w_proj.shape[1]), jnp.bfloat16),
-        in_specs=[vmem] * 4,
+        in_specs=[vmem] * 6,
         out_specs=vmem,
         scratch_shapes=[pltpu.VMEM((width // 128, length, 128), jnp.float32)],
         compiler_params=pltpu.CompilerParams(vmem_limit_bytes=48 * 2**20),
         name="mix_and_project",
-    )(heads_out, w_out, patches, w_proj)
+    )(*heads_out, *w_out, patches, w_proj)
 
 
 def on_device(
@@ -262,7 +275,10 @@
     tok_count = patches.shape[0]
     local_heads = w_qkv.shape[1] // HD
     tile = min(256, tok_count)
-    w_out_all = lax.all_gather(w_out, "tp", axis=0, tiled=True)
+    split = w_out.shape[0] // 2
+    w_out_all = [
+        lax.all_gather(part, "tp", axis=0, tiled=True) for part in (w_out[:split], w_out[split:])
+    ]
     normed = layer_norm(patches, ln_gain, ln_bias)
     grid_row, grid_col = grid_positions(segment_ids, grid_sides, split_plan[0, 0])
     quarter = HD // 4
@@ -276,18 +292,16 @@
     count = lax.axis_size("req")
     up = [(i, i + 1) for i in range(count - 1)]
     down = [(j, i) for i, j in up]
-    before = [lax.ppermute(part, "req", up) for part in (keys, values)]
-    after = [lax.ppermute(part, "req", down) for part in (keys, values)]
+    half = local_heads // 2
+    near = []
+    for first in (0, half):
+        part = jnp.stack([keys[first : first + half], values[first : first + half]])
+        near.append((lax.ppermute(part, "req", up), lax.ppermute(part, "req", down)))
     mixed_q = jnp.einsum("td,cd->ct", normed, w_qkv[0], preferred_element_type=jnp.float32)
     mixed_q = mixed_q.reshape(local_heads, HD, tok_count)
     scale = HD ** (-0.5) * 1.4426950408889634
     queries = (apply_rope(mixed_q, row_angles, col_angles, 1) * scale).astype(jnp.bfloat16)
     acc, stat = attend_own(queries, keys, values, segment_ids, tile)
-    heads_out = attend_near(queries, before, after, segment_ids, split_plan, acc, stat, tile)
-    heads_all = lax.all_gather(
-        heads_out.reshape(local_heads * HD, tok_count), "tp", axis=0, tiled=True
-    )
-    projected = mix_and_project(heads_all, w_out_all, patches, w_proj)
     per_owner = owner_dev.shape[0]
     peer_count = lax.axis_size("req")
     owner_slots = 2 * per_owner // peer_count
@@ -299,7 +313,23 @@
     slots = jnp.arange(peer_count * owner_slots, dtype=jnp.int32)
     hit = slots[:, None] == send_slot[None, :]
     send_dest = jnp.sum(jnp.where(hit, dest_row[None, :] + 1, 0), axis=1) - 1
-    got_dest = lax.all_to_all(send_dest, "req", split_axis=0, concat_axis=0, tiled=True)
+    all_dest = lax.all_gather(send_dest, "req", axis=0, tiled=True)
+    all_dest = all_dest.reshape(peer_count, peer_count, owner_slots)
+    got_dest = lax.dynamic_index_in_dim(
+        all_dest, lax.axis_index("req"), axis=1, keepdims=False
+    ).reshape(-1)
+    acc, stat, w_out_all, got_dest, near = lax.optimization_barrier(
+        (acc, stat, w_out_all, got_dest, near)
+    )
+    heads_all = []
+    for part, (before, after) in enumerate(near):
+        heads_out = attend_near(
+            queries, before, after, segment_ids, split_plan, acc, stat, tile, part
+        )
+        heads_all.append(
+            lax.all_gather(heads_out.reshape(half * HD, tok_count), "tp", axis=0, tiled=True)
+        )
+    projected = mix_and_project(heads_all, w_out_all, patches, w_proj)
     place = (jnp.arange(per_owner, dtype=jnp.int32)[:, None] == got_dest[None, :]).astype(
         jnp.bfloat16
     )

time: 211 us -> 217 us (1.028)
  blocking collectives: 0 us -> 89.4 us
  waiting for transfers between devices: 84.8 us -> 31.4 us
  starting transfers between devices: 29.7 us -> 14 us
  Pallas kernels: 54.5 us -> 44.2 us
  local copies, waits for them, and re-layouts: 6.26 us -> 10.2 us
  other arithmetic: 10.4 us -> 6.62 us
  matrix products: 10.1 us -> 7.6 us
    all_gather x0 -> x1, blocking collectives: none -> 69.2 us  [on_device(): all_dest = lax.all_gather(send_dest, 'req', axis=0, tiled=True)]
    all_gather x2 -> x4, waiting for transfers between devices: 54.9 us -> 30.6 us  [the longest x2 30.6 us: on_device(): lax.all_gather(heads_out.reshape(half * HD, tok_count), 'tp', axis=0, til...]
    all_to_all x0 -> x1, blocking collectives: none -> 20.2 us  [on_device(): lax.all_to_all(send_rows, 'req', split_axis=0, concat_axis=0, tiled=True)]
    all_to_all x2 -> x0, starting transfers between devices: 16 us -> none  [the longest x1 10.5 us: on_device(): lax.all_to_all(send_dest, 'req', split_axis=0, concat_axis=0, tiled=True)]
    ppermute x4, waiting for transfers between devices: 15.6 us -> 0.01 us  [the longest x2 0.01 us: on_device(): lax.ppermute(part, 'req', up)]
    all_to_all x2 -> x0, waiting for transfers between devices: 13.6 us -> none  [the longest x1 13.6 us: on_device(): lax.all_to_all(send_rows, 'req', split_axis=0, concat_axis=0, tiled=True)]
    pallas_call x1, Pallas kernels: 30.6 us -> 20.8 us  [attend_own(): pl.pallas_call(lambda *refs: own_kernel(tile, *refs), out_shape=(jax.Shap...]
    unnamed x26, local copies, waits for them, and re-layouts: 3.31 us -> 5.91 us
  transfers between devices with their start and end apart: 8 -> 8, of which waited for: 5 -> 2; matrix products, arithmetic and copies ran while one was open for 5% -> 7% of each run, Pallas kernels for 20% -> 12%
where the time goes in v2:
time: 217 us
  blocking collectives  89.4 us (41%)
  Pallas kernels  44.2 us (20%)
  waiting for transfers between devices  31.4 us (14%)
  starting transfers between devices  14 us (6%)
  between operations  13.4 us (6%)
  local copies, waits for them, and re-layouts  10.2 us (5%)
  matrix products  7.6 us (4%)
  other arithmetic  6.62 us (3%)
    all_gather x1, blocking collectives, on_device(): all_dest = lax.all_gather(send_dest, 'req', axis=0, tiled=True)  69.2 us
    all_gather x2, waiting for transfers between devices, on_device(): lax.all_gather(heads_out.reshape(half * HD, tok_count), 'tp', axis=0, til...  30.6 us
    pallas_call x1, Pallas kernels, attend_own(): pl.pallas_call(lambda *refs: own_kernel(tile, *refs), out_shape=(jax.Shap...  20.8 us
    all_to_all x1, blocking collectives, on_device(): lax.all_to_all(send_rows, 'req', split_axis=0, concat_axis=0, tiled=True)  20.2 us
    pallas_call x2, Pallas kernels, attend_near(): pl.pallas_call(lambda *refs: near_kernel(tile, *refs), out_shape=jax.Shap...  11.7 us
    pallas_call x1, Pallas kernels, mix_and_project(): pl.pallas_call(mix_kernel, out_shape=jax.ShapeDtypeStruct((length // 4, w...  11.6 us
    ppermute x2, starting transfers between devices, on_device(): lax.ppermute(part, 'req', up)  11.1 us
    unnamed x26, local copies, waits for them, and re-layouts  5.91 us
  transfers between devices with their start and end apart: 8, of which 2 were waited for; matrix products, arithmetic and copies ran while one was open for 7% of the time, Pallas kernels for 12%

profile of v2, /device:TPU:0, one launch (start us, length us, event | category | flops | bytes accessed | tf_op | source)
XLA Modules:
  0.0 216.9 jit_solution(7973811895704185543)
XLA Ops:
  6.5 2.4 %fusion.39 = (bf16[176,1408]{1,0:T(8,128)(2,1)}, bf16[176,1408]{1,0:T(8,128)(2,1)}) fusion(bf16[352,1408]{1,0:T(8,128)(2,1)} %param.20), kind=kLoop, calls=%fused_computation.96 | loop fusion | bytes 1982464 | tf_op jit(solution)/shard_map/slice | solution.py:280
  10.9 0.9 fusion.2
  12.3 2.7 %fusion.40 = (bf16[2,352,1024]{2,1,0:T(8,128)(2,1)S(1)}, f32[2,352,1024]{2,1,0:T(8,128)S(1)}) fusion(bf16[3,352,1408]{2,1,0:T(8,128)(2,1)S(1)} %copy-done.10, f32[1408]{0:T(1024)S(1)} %copy-done.11, f32[1408]{0:T(1024)S(1)} %copy-done.12, f32[1024]{0:T(1024)S(1)} %add_rsqrt_fusion, f32[1024]{0:T(1024)S(1)} %broadcast_multiply_fusion, ...), kind=kOutput, calls=%fused_computation.97 | convolution fusion | flops 2039414784 | bytes 9216000 | tf_op jit(solution)/shard_map/td,kcd->kct/dot_general | solution.py:288
  15.9 0.8 multiply_cosine_fusion.1
  17.3 0.9 pad_maximum_fusion.2
  18.2 5.7 %collective-permute-start.2 = (bf16[2,2,88,1024]{3,2,1,0:T(8,128)(2,1)}, bf16[2,2,88,1024]{3,2,1,0:T(8,128)(2,1)}, u32[]{:S(2)}, u32[]{:S(2)}) collective-permute-start(bf16[2,2,88,1024]{3,2,1,0:T(8,128)(2,1)} %pad_maximum_fusion.2), channel_id=1, source_target_pairs={{0,4},{4,8},{8,12},{12,16},{16,20},{20,24},{24,28},{1,5},{5,9},{9,... | collective-permute-start | bytes 2162696 | tf_op jit(solution)/shard_map/ppermute | solution.py:299
  23.9 1.3 collective-permute-start.3
  25.2 0.9 pad_maximum_fusion.1
  26.2 5.4 %collective-permute-start = (bf16[2,2,88,1024]{3,2,1,0:T(8,128)(2,1)}, bf16[2,2,88,1024]{3,2,1,0:T(8,128)(2,1)}, u32[]{:S(2)}, u32[]{:S(2)}) collective-permute-start(bf16[2,2,88,1024]{3,2,1,0:T(8,128)(2,1)} %pad_maximum_fusion.1), channel_id=1, source_target_pairs={{0,4},{4,8},{8,12},{12,16},{16,20},{20,24},{24,28},{1,5},{5,9},{9,... | collective-permute-start | bytes 2162696 | tf_op jit(solution)/shard_map/ppermute | solution.py:299
  31.6 1.3 collective-permute-start.1
  32.9 1.0 slice.130
  35.2 3.6 %fusion.15 = f32[1024,352]{0,1:T(8,128)S(1)} fusion(bf16[3,352,1408]{2,1,0:T(8,128)(2,1)} %param.19, bf16[1024,1408]{1,0:T(8,128)(2,1)} %patch_ref.1, f32[1408]{0:T(1024)S(1)} %copy-done.11, f32[1408]{0:T(1024)S(1)} %copy-done.12, f32[1024]{0:T(1024)S(1)} %add_rsqrt_fusion, f32[1024]{0:T(1024)S(1)} %broadcast_multiply_fusion), kind=kOutput, calls=%fused_computation.16 | convolution fusion | flops 1023672320 | bytes 5336064 | tf_op jit(solution)/shard_map/td,cd->ct/dot_general | solution.py:300
  38.8 69.2 %all-gather = s32[8,1,512]{2,1,0:T(1,128)S(1)} all-gather(s32[1,1,512]{2,1,0:T(1,128)S(1)} %bitcast.66), channel_id=1, replica_groups=mesh['req'=8,'tp'=4] {'req'}, dimensions={0}, use_global_device_ids=true | all-gather | bytes 18432 | tf_op jit(solution)/shard_map/all_gather | solution.py:316
  109.3 20.8 %own_attention.1 = (f32[4,88,1024]{2,1,0:T(8,128)S(1)}, f32[4,8,1024]{2,1,0:T(8,128)S(1)}) custom-call(s32[1024]{0:T(1024)S(1)} %copy-done.4, bf16[4,88,1024]{2,1,0:T(8,128)(2,1)S(1)} %fusion.14.refs_1_.refs_2_, bf16[4,88,1024]{2,1,0:T(8,128)(2,1)S(1)} %pad_maximum_fusion.refs_2_, bf16[4,88,1024]{2,1,0:T(8,128)(2,1)S(1)} %bitcast.53, ...), custom_call_target="tpu_custom_call" | custom-call | flops 1476395008 | bytes 2883584 | tf_op jit(solution)/shard_map/own_attention/pallas_call | solution.py:149
  130.2 5.9 %near_attention.3 = bf16[2,88,1024]{2,1,0:T(8,128)(2,1)} custom-call(s32[1024]{0:T(1024)S(1)} %copy-done.4, s32[1,2]{1,0:T(1,128)S(1)} %copy-done.5, bf16[4,88,1024]{2,1,0:T(8,128)(2,1)S(1)} %fusion.14.refs_1_.refs_2_, bf16[2,2,88,1024]{3,2,1,0:T(8,128)(2,1)} %collective-permute-done.2.refs_3_, bf16[2,2,88,1024]{3,2,1,0:T(8,128)(2,1)} %collective-permute-done.3.refs_4_, ...), custom_call_target="tpu_custom_call" | custom-call | flops 738197504 | bytes 2162688 | tf_op jit(solution)/shard_map/near_attention/pallas_call | solution.py:181
  136.4 5.9 %near_attention.2 = bf16[2,88,1024]{2,1,0:T(8,128)(2,1)} custom-call(s32[1024]{0:T(1024)S(1)} %copy-done.4, s32[1,2]{1,0:T(1,128)S(1)} %copy-done.5, bf16[4,88,1024]{2,1,0:T(8,128)(2,1)S(1)} %fusion.14.refs_1_.refs_2_, bf16[2,2,88,1024]{3,2,1,0:T(8,128)(2,1)} %collective-permute-done.refs_3_, bf16[2,2,88,1024]{3,2,1,0:T(8,128)(2,1)} %collective-permute-done.1.refs_4_, ...), custom_call_target="tpu_custom_call" | custom-call | flops 738197504 | bytes 2162688 | tf_op jit(solution)/shard_map/near_attention/pallas_call | solution.py:181
  142.3 10.2 %all-gather.12.cloned.1.call-done.ho_b_ref = bf16[704,1024]{1,0:T(8,128)(2,1)} async-done(((bf16[176,1024]{1,0:T(8,128)(2,1)}), bf16[704,1024]{1,0:T(8,128)(2,1)}) %all-gather.12.cloned.1.call-update) | async-done | bytes 1441808 | tf_op jit(solution)/shard_map/all_gather | solution.py:330
  152.5 20.4 %all-gather.10.cloned.1.call-done.ho_a_ref = bf16[704,1024]{1,0:T(8,128)(2,1)} async-done(((bf16[176,1024]{1,0:T(8,128)(2,1)}), bf16[704,1024]{1,0:T(8,128)(2,1)}) %all-gather.10.cloned.1.call-update) | async-done | bytes 1441808 | tf_op jit(solution)/shard_map/all_gather | solution.py:330
  172.9 1.5 copy-done
  174.4 1.4 copy-done.1
  175.8 1.4 copy-done.2
  177.2 11.6 %mix_and_project.1 = bf16[256,512]{1,0:T(8,128)(2,1)S(1)} custom-call(bf16[704,1024]{1,0:T(8,128)(2,1)S(1)} %copy-done.2, bf16[704,1024]{1,0:T(8,128)(2,1)S(1)} %copy-done.1, bf16[704,1408]{1,0:T(8,128)(2,1)S(1)} %copy-done, bf16[704,1408]{1,0:T(8,128)(2,1)} %all-gather.8.cloned.1.call-done.wb_ref, bf16[1024,1408]{1,0:T(8,128)(2,1)} %patch_ref.1, ...), custom_call_target="tpu_custom_call" | custom-call | tf_op jit(solution)/shard_map/mix_and_project/pallas_call | solution.py:251
  189.1 20.2 %all_to_all.12 = bf16[8,64,512]{2,1,0:T(8,128)(2,1)S(1)} all-to-all(bf16[8,64,512]{2,1,0:T(8,128)(2,1)S(1)} %bitcast.60), channel_id=1, replica_groups=mesh['req'=8,'tp'=4] {'req'}, dimensions={0} | all-to-all | bytes 1048576 | tf_op jit(solution)/shard_map/all_to_all | solution.py:339
  209.3 1.0 convolution_convert_fusion.1
  (70 shorter events, 7.2 us)
Async XLA Ops:
  6.5 3.2 %copy-start.4 = (s32[1024]{0:T(1024)S(1)}, s32[1024]{0:T(1024)}, u32[]{:S(2)}) copy-start(s32[1024]{0:T(1024)} %refs_0_.5) | copy-start | bytes 12292
  6.5 3.9 %copy-start.6 = (bf16[1024,1408]{1,0:T(8,128)(2,1)S(1)}, bf16[1024,1408]{1,0:T(8,128)(2,1)}, u32[]{:S(2)}) copy-start(bf16[1024,1408]{1,0:T(8,128)(2,1)} %patch_ref.1) | copy-start | bytes 8650756
  6.5 123.7 %all-gather.6.cloned.1.call-start = ((), (), s32[]{:S(2)}) async-start(), calls=%async_computation.1 | async-start | bytes 2478080 | tf_op jit(solution)/shard_map/all_gather | solution.py:280
  8.9 121.3 %all-gather.8.cloned.1.call-start = ((), (), s32[]{:S(2)}) async-start(), calls=%async_computation.2 | async-start | bytes 2478080 | tf_op jit(solution)/shard_map/all_gather | solution.py:280
  9.7 142.8 %all-gather.12.cloned.1.call-start = ((), (), s32[]{:S(2)}) async-start(), calls=%async_computation.4 | async-start | bytes 1802240 | tf_op jit(solution)/shard_map/all_gather | solution.py:330
  10.4 1.8 copy-start.10
  10.4 1.8 copy-start.11
  10.4 1.8 copy-start.12
  15.0 0.7 copy-start.5
  15.0 0.7 copy-start.8
  17.2 16.9 %copy-start.7 = (s32[256]{0:T(256)S(1)}, s32[256]{0:T(256)}, u32[]{:S(2)}) copy-start(s32[256]{0:T(256)} %param.15) | copy-start | bytes 3076
  17.3 17.8 %copy-start.9 = (s32[256]{0:T(256)S(1)}, s32[256]{0:T(256)}, u32[]{:S(2)}) copy-start(s32[256]{0:T(256)} %param.16) | copy-start | bytes 3076
  18.2 111.9 %collective-permute-start.2 = (bf16[2,2,88,1024]{3,2,1,0:T(8,128)(2,1)}, bf16[2,2,88,1024]{3,2,1,0:T(8,128)(2,1)}, u32[]{:S(2)}, u32[]{:S(2)}) collective-permute-start(bf16[2,2,88,1024]{3,2,1,0:T(8,128)(2,1)} %pad_maximum_fusion.2), channel_id=1, source_target_pairs={{0,4},{4,8},{8,12},{12,16},{16,20},{20,24},{24,28},{1,5},{5,9},{9,... | collective-permute-start | bytes 2162696 | tf_op jit(solution)/shard_map/ppermute | solution.py:299
  23.9 106.2 %collective-permute-start.3 = (bf16[2,2,88,1024]{3,2,1,0:T(8,128)(2,1)}, bf16[2,2,88,1024]{3,2,1,0:T(8,128)(2,1)}, u32[]{:S(2)}, u32[]{:S(2)}) collective-permute-start(bf16[2,2,88,1024]{3,2,1,0:T(8,128)(2,1)} %pad_maximum_fusion.2), channel_id=1, source_target_pairs={{4,0},{8,4},{12,8},{16,12},{20,16},{24,20},{28,24},{5,1},{9,5},{13... | collective-permute-start | bytes 2162696 | tf_op jit(solution)/shard_map/ppermute | solution.py:299
  26.2 104.0 %collective-permute-start = (bf16[2,2,88,1024]{3,2,1,0:T(8,128)(2,1)}, bf16[2,2,88,1024]{3,2,1,0:T(8,128)(2,1)}, u32[]{:S(2)}, u32[]{:S(2)}) collective-permute-start(bf16[2,2,88,1024]{3,2,1,0:T(8,128)(2,1)} %pad_maximum_fusion.1), channel_id=1, source_target_pairs={{0,4},{4,8},{8,12},{12,16},{16,20},{20,24},{24,28},{1,5},{5,9},{9,... | collective-permute-start | bytes 2162696 | tf_op jit(solution)/shard_map/ppermute | solution.py:299
  31.6 98.6 %collective-permute-start.1 = (bf16[2,2,88,1024]{3,2,1,0:T(8,128)(2,1)}, bf16[2,2,88,1024]{3,2,1,0:T(8,128)(2,1)}, u32[]{:S(2)}, u32[]{:S(2)}) collective-permute-start(bf16[2,2,88,1024]{3,2,1,0:T(8,128)(2,1)} %pad_maximum_fusion.1), channel_id=1, source_target_pairs={{4,0},{8,4},{12,8},{16,12},{20,16},{24,20},{28,24},{5,1},{9,5},{13... | collective-permute-start | bytes 2162696 | tf_op jit(solution)/shard_map/ppermute | solution.py:299
  108.2 1.1 copy-start.3
  136.1 36.8 %all-gather.10.cloned.1.call-start = ((), (), s32[]{:S(2)}) async-start(), calls=%async_computation.3 | async-start | bytes 1802240 | tf_op jit(solution)/shard_map/all_gather | solution.py:330
  172.9 1.6 copy-start
  174.4 1.4 copy-start.1
  175.8 1.4 copy-start.2
Sparse Core Ops, SparseCore 0:
  9.1 24.7 all-gather.5
  35.4 21.8 all-gather.7
  136.3 16.2 all-gather.11
  153.9 18.9 all-gather.9

commit v3 on v2

--- a/solution.py
+++ b/solution.py
@@ -313,13 +313,8 @@
     slots = jnp.arange(peer_count * owner_slots, dtype=jnp.int32)
     hit = slots[:, None] == send_slot[None, :]
     send_dest = jnp.sum(jnp.where(hit, dest_row[None, :] + 1, 0), axis=1) - 1
-    all_dest = lax.all_gather(send_dest, "req", axis=0, tiled=True)
-    all_dest = all_dest.reshape(peer_count, peer_count, owner_slots)
-    got_dest = lax.dynamic_index_in_dim(
-        all_dest, lax.axis_index("req"), axis=1, keepdims=False
-    ).reshape(-1)
-    acc, stat, w_out_all, got_dest, near = lax.optimization_barrier(
-        (acc, stat, w_out_all, got_dest, near)
+    acc, stat, w_out_all, near = lax.optimization_barrier(
+        (acc, stat, w_out_all, near)
     )
     heads_all = []
     for part, (before, after) in enumerate(near):
@@ -330,6 +325,7 @@
             lax.all_gather(heads_out.reshape(half * HD, tok_count), "tp", axis=0, tiled=True)
         )
     projected = mix_and_project(heads_all, w_out_all, patches, w_proj)
+    got_dest = lax.all_to_all(send_dest, "req", split_axis=0, concat_axis=0, tiled=True)
     place = (jnp.arange(per_owner, dtype=jnp.int32)[:, None] == got_dest[None, :]).astype(
         jnp.bfloat16
     )

time: 217 us -> 184 us (0.85)
  blocking collectives: 89.4 us -> 0 us
  waiting for transfers between devices: 31.4 us -> 62.8 us
  starting transfers between devices: 14 us -> 32.8 us
  local copies, waits for them, and re-layouts: 10.2 us -> 12.6 us
    all_gather x1 -> x0, blocking collectives: 69.2 us -> none  [on_device(): all_dest = lax.all_gather(send_dest, 'req', axis=0, tiled=True)]
    ppermute x2, waiting for transfers between devices: 0.01 us -> 25.4 us  [on_device(): lax.ppermute(part, 'req', up)]
    all_to_all x1 -> x0, blocking collectives: 20.2 us -> none  [on_device(): lax.all_to_all(send_rows, 'req', split_axis=0, concat_axis=0, tiled=True)]
    all_to_all x0 -> x2, starting transfers between devices: none -> 18.7 us  [the longest x1 13.2 us: on_device(): lax.all_to_all(send_dest, 'req', split_axis=0, concat_axis=0, tiled=True)]
    all_to_all x0 -> x2, waiting for transfers between devices: none -> 13.6 us  [the longest x1 13.6 us: on_device(): lax.all_to_all(send_rows, 'req', split_axis=0, concat_axis=0, tiled=True)]
    all_gather x2, waiting for transfers between devices: 30.6 us -> 23 us  [on_device(): lax.all_gather(heads_out.reshape(half * HD, tok_count), 'tp', axis=0, til...]
    unnamed x26 -> x38, local copies, waits for them, and re-layouts: 5.91 us -> 5.71 us
  transfers between devices with their start and end apart: 8 -> 10, of which waited for: 2 -> 5; matrix products, arithmetic and copies ran while one was open for 7% -> 12% of each run, Pallas kernels for 12% -> 21%
where the time goes in v3:
time: 184 us
  waiting for transfers between devices  62.8 us (34%)
  Pallas kernels  44.1 us (24%)
  starting transfers between devices  32.8 us (18%)
  between operations  13.4 us (7%)
  local copies, waits for them, and re-layouts  12.6 us (7%)
  matrix products  9.58 us (5%)
  other arithmetic  8.42 us (5%)
    ppermute x2, waiting for transfers between devices, on_device(): lax.ppermute(part, 'req', up)  25.4 us
    all_gather x2, waiting for transfers between devices, on_device(): lax.all_gather(heads_out.reshape(half * HD, tok_count), 'tp', axis=0, til...  23 us
    pallas_call x1, Pallas kernels, attend_own(): pl.pallas_call(lambda *refs: own_kernel(tile, *refs), out_shape=(jax.Shap...  20.8 us
    all_to_all x1, waiting for transfers between devices, on_device(): lax.all_to_all(send_rows, 'req', split_axis=0, concat_axis=0, tiled=True)  13.6 us
    all_to_all x1, starting transfers between devices, on_device(): lax.all_to_all(send_dest, 'req', split_axis=0, concat_axis=0, tiled=True)  13.2 us
    pallas_call x2, Pallas kernels, attend_near(): pl.pallas_call(lambda *refs: near_kernel(tile, *refs), out_shape=jax.Shap...  11.7 us
    pallas_call x1, Pallas kernels, mix_and_project(): pl.pallas_call(mix_kernel, out_shape=jax.ShapeDtypeStruct((length // 4, w...  11.6 us
    ppermute x2, starting transfers between devices, on_device(): lax.ppermute(part, 'req', up)  11.2 us
  transfers between devices with their start and end apart: 10, of which 5 were waited for; matrix products, arithmetic and copies ran while one was open for 12% of the time, Pallas kernels for 21%

profile of v3, /device:TPU:0, one launch (start us, length us, event | category | flops | bytes accessed | tf_op | source)
XLA Modules:
  0.0 183.7 jit_solution(16590062837014330648)
XLA Ops:
  6.5 2.4 %fusion.39 = (bf16[176,1408]{1,0:T(8,128)(2,1)}, bf16[176,1408]{1,0:T(8,128)(2,1)}) fusion(bf16[352,1408]{1,0:T(8,128)(2,1)} %param.20), kind=kLoop, calls=%fused_computation.95 | loop fusion | bytes 1982464 | tf_op jit(solution)/shard_map/slice | solution.py:280
  11.7 4.7 %fusion.40 = (bf16[2,352,1024]{2,1,0:T(8,128)(2,1)}, f32[2,352,1024]{2,1,0:T(8,128)}) fusion(bf16[3,352,1408]{2,1,0:T(8,128)(2,1)S(1)} %copy-done.16, f32[1408]{0:T(1024)S(1)} %copy-done.17, f32[1408]{0:T(1024)S(1)} %copy-done.18, f32[1024]{0:T(1024)S(1)} %add_rsqrt_fusion, f32[1024]{0:T(1024)S(1)} %broadcast_multiply_fusion, ...), kind=kOutput, calls=%fused_computation.96 | convolution fusion | flops 2039414784 | bytes 9216000 | tf_op jit(solution)/shard_map/td,kcd->kct/dot_general | solution.py:288
  16.8 1.6 slice.126
  22.1 5.8 %collective-permute-start.2 = (bf16[2,2,88,1024]{3,2,1,0:T(8,128)(2,1)}, bf16[2,2,88,1024]{3,2,1,0:T(8,128)(2,1)}, u32[]{:S(2)}, u32[]{:S(2)}) collective-permute-start(bf16[2,2,88,1024]{3,2,1,0:T(8,128)(2,1)} %pad_maximum_fusion.2), channel_id=1, source_target_pairs={{0,4},{4,8},{8,12},{12,16},{16,20},{20,24},{24,28},{1,5},{5,9},{9,... | collective-permute-start | bytes 2162696 | tf_op jit(solution)/shard_map/ppermute | solution.py:299
  27.8 1.3 collective-permute-start.3
  30.1 5.4 %collective-permute-start = (bf16[2,2,88,1024]{3,2,1,0:T(8,128)(2,1)}, bf16[2,2,88,1024]{3,2,1,0:T(8,128)(2,1)}, u32[]{:S(2)}, u32[]{:S(2)}) collective-permute-start(bf16[2,2,88,1024]{3,2,1,0:T(8,128)(2,1)} %pad_maximum_fusion.1), channel_id=1, source_target_pairs={{0,4},{4,8},{8,12},{12,16},{16,20},{20,24},{24,28},{1,5},{5,9},{9,... | collective-permute-start | bytes 2162696 | tf_op jit(solution)/shard_map/ppermute | solution.py:299
  35.5 1.5 collective-permute-start.1
  37.0 2.8 %fusion.15 = f32[1024,352]{0,1:T(8,128)S(1)} fusion(bf16[3,352,1408]{2,1,0:T(8,128)(2,1)} %param.19, bf16[1024,1408]{1,0:T(8,128)(2,1)S(1)} %copy-done.7, f32[1408]{0:T(1024)S(1)} %copy-done.17, f32[1408]{0:T(1024)S(1)} %copy-done.18, f32[1024]{0:T(1024)S(1)} %add_rsqrt_fusion, f32[1024]{0:T(1024)S(1)} %broadcast_multiply_fusion), kind=kOutput, calls=%fused_computation.16 | convolution fusion | flops 1023672320 | bytes 5336064 | tf_op jit(solution)/shard_map/td,cd->ct/dot_general | solution.py:300
  41.0 1.5 multiply_subtract_fusion.1
  42.7 20.8 %own_attention.1 = (f32[4,88,1024]{2,1,0:T(8,128)S(1)}, f32[4,8,1024]{2,1,0:T(8,128)S(1)}) custom-call(s32[1024]{0:T(1024)S(1)} %copy-done.4, bf16[4,88,1024]{2,1,0:T(8,128)(2,1)S(1)} %fusion.14.refs_1_.refs_2_, bf16[4,88,1024]{2,1,0:T(8,128)(2,1)S(1)} %pad_maximum_fusion.refs_2_, bf16[4,88,1024]{2,1,0:T(8,128)(2,1)S(1)} %bitcast.54, ...), custom_call_target="tpu_custom_call" | custom-call | flops 1476395008 | bytes 2883584 | tf_op jit(solution)/shard_map/own_attention/pallas_call | solution.py:149
  63.5 11.2 %collective-permute-done.2.refs_3_ = bf16[2,2,88,1024]{3,2,1,0:T(8,128)(2,1)} collective-permute-done((bf16[2,2,88,1024]{3,2,1,0:T(8,128)(2,1)}, bf16[2,2,88,1024]{3,2,1,0:T(8,128)(2,1)}, u32[]{:S(2)}, u32[]{:S(2)}) %collective-permute-start.2) | collective-permute-done | bytes 720928 | tf_op jit(solution)/shard_map/ppermute | solution.py:299
  74.7 14.3 %collective-permute-done.refs_3_ = bf16[2,2,88,1024]{3,2,1,0:T(8,128)(2,1)} collective-permute-done((bf16[2,2,88,1024]{3,2,1,0:T(8,128)(2,1)}, bf16[2,2,88,1024]{3,2,1,0:T(8,128)(2,1)}, u32[]{:S(2)}, u32[]{:S(2)}) %collective-permute-start) | collective-permute-done | bytes 720928 | tf_op jit(solution)/shard_map/ppermute | solution.py:299
  89.0 5.9 %near_attention.3 = bf16[2,88,1024]{2,1,0:T(8,128)(2,1)} custom-call(s32[1024]{0:T(1024)S(1)} %copy-done.4, s32[1,2]{1,0:T(1,128)S(1)} %copy-done.5, bf16[4,88,1024]{2,1,0:T(8,128)(2,1)S(1)} %fusion.14.refs_1_.refs_2_, bf16[2,2,88,1024]{3,2,1,0:T(8,128)(2,1)} %collective-permute-done.2.refs_3_, bf16[2,2,88,1024]{3,2,1,0:T(8,128)(2,1)} %collective-permute-done.3.refs_4_, ...), custom_call_target="tpu_custom_call" | custom-call | flops 738197504 | bytes 2162688 | tf_op jit(solution)/shard_map/near_attention/pallas_call | solution.py:181
  94.9 5.9 %near_attention.2 = bf16[2,88,1024]{2,1,0:T(8,128)(2,1)} custom-call(s32[1024]{0:T(1024)S(1)} %copy-done.4, s32[1,2]{1,0:T(1,128)S(1)} %copy-done.5, bf16[4,88,1024]{2,1,0:T(8,128)(2,1)S(1)} %fusion.14.refs_1_.refs_2_, bf16[2,2,88,1024]{3,2,1,0:T(8,128)(2,1)} %collective-permute-done.refs_3_, bf16[2,2,88,1024]{3,2,1,0:T(8,128)(2,1)} %collective-permute-done.1.refs_4_, ...), custom_call_target="tpu_custom_call" | custom-call | flops 738197504 | bytes 2162688 | tf_op jit(solution)/shard_map/near_attention/pallas_call | solution.py:181
  102.6 13.2 %all-to-all-start = ((s32[8,64,1]{1,2,0:T(1,128)}), s32[8,64,1]{1,2,0:T(1,128)S(1)}, u32[]{:S(2)}, u32[]{:S(2)}) async-start(s32[8,64,1]{1,2,0:T(1,128)} %bitcast.3), calls=%async_computation | async-start | bytes 8192 | tf_op jit(solution)/shard_map/all_to_all | solution.py:328
  115.8 2.6 %all-gather.11.cloned.1.call-done.ho_b_ref = bf16[704,1024]{1,0:T(8,128)(2,1)} async-done(((bf16[176,1024]{1,0:T(8,128)(2,1)}), bf16[704,1024]{1,0:T(8,128)(2,1)}) %all-gather.11.cloned.1.call-update) | async-done | bytes 1441808 | tf_op jit(solution)/shard_map/all_gather | solution.py:325
  118.4 20.4 %all-gather.9.cloned.1.call-done.ho_a_ref = bf16[704,1024]{1,0:T(8,128)(2,1)} async-done(((bf16[176,1024]{1,0:T(8,128)(2,1)}), bf16[704,1024]{1,0:T(8,128)(2,1)}) %all-gather.9.cloned.1.call-update) | async-done | bytes 1441808 | tf_op jit(solution)/shard_map/all_gather | solution.py:325
  138.8 1.5 copy-done
  140.3 1.4 copy-done.1
  141.7 1.4 copy-done.2
  143.0 11.6 %mix_and_project.1 = bf16[256,512]{1,0:T(8,128)(2,1)S(1)} custom-call(bf16[704,1024]{1,0:T(8,128)(2,1)S(1)} %copy-done.2, bf16[704,1024]{1,0:T(8,128)(2,1)S(1)} %copy-done.1, bf16[704,1408]{1,0:T(8,128)(2,1)S(1)} %copy-done, bf16[704,1408]{1,0:T(8,128)(2,1)} %all-gather.7.cloned.1.call-done.wb_ref, bf16[1024,1408]{1,0:T(8,128)(2,1)} %patch_ref.1, ...), custom_call_target="tpu_custom_call" | custom-call | tf_op jit(solution)/shard_map/mix_and_project/pallas_call | solution.py:251
  154.6 1.1 convolution_convert_fusion
  155.8 5.5 %all-to-all-start.1 = ((bf16[8,64,512]{2,1,0:T(8,128)(2,1)}), bf16[8,64,512]{2,1,0:T(8,128)(2,1)S(1)}, u32[]{:S(2)}, u32[]{:S(2)}) async-start(bf16[8,64,512]{2,1,0:T(8,128)(2,1)} %bitcast.23), calls=%async_computation.1 | async-start | bytes 1048576 | tf_op jit(solution)/shard_map/all_to_all | solution.py:335
  162.5 13.6 %all-to-all-done.1 = bf16[8,64,512]{2,1,0:T(8,128)(2,1)S(1)} async-done(((bf16[8,64,512]{2,1,0:T(8,128)(2,1)}), bf16[8,64,512]{2,1,0:T(8,128)(2,1)S(1)}, u32[]{:S(2)}, u32[]{:S(2)}) %all-to-all-start.1) | async-done | bytes 524320 | tf_op jit(solution)/shard_map/all_to_all | solution.py:335
  (85 shorter events, 13.2 us)
Async XLA Ops:
  6.5 3.2 %copy-start.4 = (s32[1024]{0:T(1024)S(1)}, s32[1024]{0:T(1024)}, u32[]{:S(2)}) copy-start(s32[1024]{0:T(1024)} %refs_0_.5) | copy-start | bytes 12292
  6.5 3.3 %copy-start.6 = (bf16[1024,1408]{1,0:T(8,128)(2,1)S(1)}, bf16[1024,1408]{1,0:T(8,128)(2,1)}, u32[]{:S(2)}) copy-start(bf16[1024,1408]{1,0:T(8,128)(2,1)} %patch_ref.1) | copy-start | bytes 8650756
  6.5 82.4 %all-gather.5.cloned.1.call-start = ((), (), s32[]{:S(2)}) async-start(), calls=%async_computation.2 | async-start | bytes 2478080 | tf_op jit(solution)/shard_map/all_gather | solution.py:280
  8.9 80.1 %all-gather.7.cloned.1.call-start = ((), (), s32[]{:S(2)}) async-start(), calls=%async_computation.3 | async-start | bytes 2478080 | tf_op jit(solution)/shard_map/all_gather | solution.py:280
  9.7 108.7 %all-gather.11.cloned.1.call-start = ((), (), s32[]{:S(2)}) async-start(), calls=%async_computation.5 | async-start | bytes 1802240 | tf_op jit(solution)/shard_map/all_gather | solution.py:325
  9.8 1.8 %copy-start.16 = (bf16[3,352,1408]{2,1,0:T(8,128)(2,1)S(1)}, bf16[3,352,1408]{2,1,0:T(8,128)(2,1)}, u32[]{:S(2)}) copy-start(bf16[3,352,1408]{2,1,0:T(8,128)(2,1)} %param.19) | copy-start | bytes 8921092
  9.8 1.8 %copy-start.17 = (f32[1408]{0:T(1024)S(1)}, f32[1408]{0:T(1024)}, u32[]{:S(2)}) copy-start(f32[1408]{0:T(1024)} %param.18) | copy-start | bytes 16900
  9.8 1.8 %copy-start.18 = (f32[1408]{0:T(1024)S(1)}, f32[1408]{0:T(1024)}, u32[]{:S(2)}) copy-start(f32[1408]{0:T(1024)} %param.17) | copy-start | bytes 16900
  16.3 2.2 %copy-start.5 = (s32[1,2]{1,0:T(1,128)S(1)}, s32[1,2]{1,0:T(1,128)}, u32[]{:S(2)}) copy-start(s32[1,2]{1,0:T(1,128)} %refs_1_.3) | copy-start | bytes 28
  16.3 2.2 %copy-start.14 = (s32[1024]{0:T(1024)S(1)}, s32[1024]{0:T(1024)}, u32[]{:S(2)}) copy-start(s32[1024]{0:T(1024)} %param.13) | copy-start | bytes 12292
  19.5 1.6 copy-start.9
  19.5 1.6 copy-start.10
  19.6 1.6 copy-start.11
  20.1 16.9 %copy-start.7 = (bf16[1024,1408]{1,0:T(8,128)(2,1)S(1)}, bf16[1024,1408]{1,0:T(8,128)(2,1)}, u32[]{:S(2)}) copy-start(bf16[1024,1408]{1,0:T(8,128)(2,1)} %patch_ref.1) | copy-start | bytes 8650756
  22.1 52.6 %collective-permute-start.2 = (bf16[2,2,88,1024]{3,2,1,0:T(8,128)(2,1)}, bf16[2,2,88,1024]{3,2,1,0:T(8,128)(2,1)}, u32[]{:S(2)}, u32[]{:S(2)}) collective-permute-start(bf16[2,2,88,1024]{3,2,1,0:T(8,128)(2,1)} %pad_maximum_fusion.2), channel_id=1, source_target_pairs={{0,4},{4,8},{8,12},{12,16},{16,20},{20,24},{24,28},{1,5},{5,9},{9,... | collective-permute-start | bytes 2162696 | tf_op jit(solution)/shard_map/ppermute | solution.py:299
  27.8 46.9 %collective-permute-start.3 = (bf16[2,2,88,1024]{3,2,1,0:T(8,128)(2,1)}, bf16[2,2,88,1024]{3,2,1,0:T(8,128)(2,1)}, u32[]{:S(2)}, u32[]{:S(2)}) collective-permute-start(bf16[2,2,88,1024]{3,2,1,0:T(8,128)(2,1)} %pad_maximum_fusion.2), channel_id=1, source_target_pairs={{4,0},{8,4},{12,8},{16,12},{20,16},{24,20},{28,24},{5,1},{9,5},{13... | collective-permute-start | bytes 2162696 | tf_op jit(solution)/shard_map/ppermute | solution.py:299
  30.1 58.9 %collective-permute-start = (bf16[2,2,88,1024]{3,2,1,0:T(8,128)(2,1)}, bf16[2,2,88,1024]{3,2,1,0:T(8,128)(2,1)}, u32[]{:S(2)}, u32[]{:S(2)}) collective-permute-start(bf16[2,2,88,1024]{3,2,1,0:T(8,128)(2,1)} %pad_maximum_fusion.1), channel_id=1, source_target_pairs={{0,4},{4,8},{8,12},{12,16},{16,20},{20,24},{24,28},{1,5},{5,9},{9,... | collective-permute-start | bytes 2162696 | tf_op jit(solution)/shard_map/ppermute | solution.py:299
  35.5 53.4 %collective-permute-start.1 = (bf16[2,2,88,1024]{3,2,1,0:T(8,128)(2,1)}, bf16[2,2,88,1024]{3,2,1,0:T(8,128)(2,1)}, u32[]{:S(2)}, u32[]{:S(2)}) collective-permute-start(bf16[2,2,88,1024]{3,2,1,0:T(8,128)(2,1)} %pad_maximum_fusion.1), channel_id=1, source_target_pairs={{4,0},{8,4},{12,8},{16,12},{20,16},{24,20},{28,24},{5,1},{9,5},{13... | collective-permute-start | bytes 2162696 | tf_op jit(solution)/shard_map/ppermute | solution.py:299
  41.0 1.7 copy-start.3
  94.8 6.0 %copy-start.13 = (s32[256]{0:T(256)S(1)}, s32[256]{0:T(256)}, u32[]{:S(2)}) copy-start(s32[256]{0:T(256)} %param.15) | copy-start | bytes 3076
  94.8 6.9 %copy-start.15 = (s32[256]{0:T(256)S(1)}, s32[256]{0:T(256)}, u32[]{:S(2)}) copy-start(s32[256]{0:T(256)} %param.16) | copy-start | bytes 3076
  94.9 43.9 %all-gather.9.cloned.1.call-start = ((), (), s32[]{:S(2)}) async-start(), calls=%async_computation.4 | async-start | bytes 1802240 | tf_op jit(solution)/shard_map/all_gather | solution.py:325
  102.6 53.2 %all-to-all-start = ((s32[8,64,1]{1,2,0:T(1,128)}), s32[8,64,1]{1,2,0:T(1,128)S(1)}, u32[]{:S(2)}, u32[]{:S(2)}) async-start(s32[8,64,1]{1,2,0:T(1,128)} %bitcast.3), calls=%async_computation | async-start | bytes 8192 | tf_op jit(solution)/shard_map/all_to_all | solution.py:328
  155.8 20.4 %all-to-all-start.1 = ((bf16[8,64,512]{2,1,0:T(8,128)(2,1)}), bf16[8,64,512]{2,1,0:T(8,128)(2,1)S(1)}, u32[]{:S(2)}, u32[]{:S(2)}) async-start(bf16[8,64,512]{2,1,0:T(8,128)(2,1)} %bitcast.23), calls=%async_computation.1 | async-start | bytes 1048576 | tf_op jit(solution)/shard_map/all_to_all | solution.py:335
  (5 other events, 7.4 us)
Sparse Core Ops, SparseCore 0:
  9.0 24.6 all-gather.4
  35.3 21.9 all-gather.6
  95.0 23.3 all-gather.10
  119.8 18.9 all-gather.8
